TPU v7x, 128 devices: a whole 4x4x4 slice. The times are simulated.
128 devices in a mesh: ctx: 32 (over z, y, x_lo), wa: 4 (over x_hi, core).
Axes of the slice: x: 4 (x_hi: 2, x_lo: 2; x = x_hi * 2 + x_lo), y: 4, z: 4, core: 2. Of those that a mesh axis runs over, the one named last changes fastest.
Arguments:
- tokens: bfloat16 [8192, 1024], P('ctx'), may hold values from -6 to 6
- cotangent: bfloat16 [8192, 1024], P('ctx'), may hold values from -6 to 6
- pairing: int32 [32], replicated, may hold values from 0 to 31, each once
- routes: int32 [8192, 8], P('ctx'), may hold values from 0 to 15, all different within a row
- norm_attn: float32 [1024], replicated, may hold values from 0.25 to 1.75
- w_query: bfloat16 [1024, 1024], P(None, 'wa'), may hold values from -0.1875 to 0.1875
- w_key: bfloat16 [1024, 512], P(None, 'wa'), may hold values from -0.1875 to 0.1875
- w_value: bfloat16 [1024, 512], P(None, 'wa'), may hold values from -0.1875 to 0.1875
- w_out: bfloat16 [1024, 1024], P('wa'), may hold values from -1.5 to 1.5
- norm_moe: float32 [1024], replicated, may hold values from 0.25 to 1.75
- w_router: bfloat16 [1024, 16], replicated, may hold values from -0.09375 to 0.09375
- w_gate: bfloat16 [16, 1024, 512], P('wa'), may hold values from -0.1875 to 0.1875
- w_up: bfloat16 [16, 1024, 512], P('wa'), may hold values from -0.1875 to 0.1875
- w_down: bfloat16 [16, 512, 1024], P('wa'), may hold values from -0.5 to 0.5
Outputs:
- output: bfloat16 [8192, 1024], P('ctx')
- grad_tokens: bfloat16 [8192, 1024], P('ctx')
- grad_norm_attn: float32 [1024], P('ctx')
- grad_query: float32 [1024, 1024], P('ctx', 'wa')
- grad_key: float32 [1024, 512], P('ctx', 'wa')
- grad_value: float32 [1024, 512], P('ctx', 'wa')
- grad_out: float32 [1024, 1024], P('wa', 'ctx')
- grad_norm_moe: float32 [1024], P('ctx')
- grad_router: float32 [1024, 16], P('ctx')
- grad_gate: float32 [16, 1024, 512], P('wa', 'ctx')
- grad_up: float32 [16, 1024, 512], P('wa', 'ctx')
- grad_down: float32 [16, 512, 1024], P('wa', 'ctx')
Inputs may be any that keep to these rules, and one draw needn't show every extreme that they name: `pairing`: a permutation. `routes`: each row names 8 different experts, and every expert is named somewhere.
All inputs are finite; a program needn't handle non-finite values.
Results may differ from a plain program's by a relative error of at most 0.033.
Values may be sent and summed in bfloat16 or wider, within the bound.
No kernel may reach another device: no remote copies, remote signals or barrier semaphores. Data moves between devices by JAX's collectives and lax.ppermute only.
A program may use at most 128 MiB of HBM per device.

v0:
```python
import jax
import jax.numpy as jnp
from jax import lax
from jax.experimental import pallas as pl
from jax.experimental.pallas import tpu as pltpu
from jax.sharding import Mesh
from jax.sharding import PartitionSpec as P

HEAD_DIM = 64
EPS = 1e-05
THETA = 10000.0
CTX = ("z", "y", "xl")
WA = ("xh", "c")
ZY = ("z", "y")
CHIPS = ("xl", "xh")
BF16 = jnp.bfloat16
F32 = jnp.float32
SWAP = [(0, 1), (1, 0)]


def dot(left, right):
    return jnp.dot(left, right, preferred_element_type=F32)


def outer(left, right):
    return lax.dot_general(left, right, (((0,), (0,)), ((), ())), preferred_element_type=F32)


def inner(left, right):
    return lax.dot_general(left, right, (((1,), (1,)), ((), ())), preferred_element_type=F32)


def rms(values, gain):
    factor = lax.rsqrt(jnp.mean(values * values, -1, keepdims=True) + EPS)
    return values * factor * gain, factor


def swap_x(mine):
    other = lax.ppermute(mine, "xl", SWAP)
    low = lax.axis_index("xl") == 0
    return jnp.concatenate([jnp.where(low, mine, other), jnp.where(low, other, mine)], 0)


TILE = 512
LIMIT = 48 * 1024 * 1024


def full_turn(flat, cosine, sine):
    rows, width = flat.shape
    lane = lax.broadcasted_iota(jnp.int32, (rows, 128), 1)
    first = (lane & 63) < 32
    parts = []
    for n in range(width // 128):
        piece = flat[:, n * 128 : (n + 1) * 128]
        other = jnp.where(first, pltpu.roll(piece, 96, 1), pltpu.roll(piece, 32, 1))
        parts.append(piece * cosine + other * sine)
    return parts[0] if len(parts) == 1 else jnp.concatenate(parts, 1)


def lane_angles(pos):
    lane = jnp.arange(128, dtype=jnp.int32)
    freq = THETA ** (-((lane % 32).astype(F32) * 2.0 / HEAD_DIM))
    angle = pos.astype(F32)[:, None] * freq[None, :]
    sign = jnp.where(lane % 64 < 32, -1.0, 1.0)
    return jnp.cos(angle), jnp.sin(angle) * sign[None, :]


def heads_across(block, low):
    turned = block.T
    both = jnp.concatenate([turned[:64], turned[64:]], 1)
    zero = jnp.zeros_like(both)
    return jnp.concatenate([both, zero] if low == 0 else [zero, both], 0)


def heads_back(both):
    return jnp.concatenate([both[:, :128], both[:, 128:]], 0).T


def attend_kernel(place, slot, q_ref, kv_ref, low_ref, o_ref, lse_ref, ks_ref, kt_ref):
    per = TILE // 128

    def sort(tile, unused):
        for j in range(per):
            block = kv_ref[slot[tile * per + j]]
            ks_ref[tile, j * 128 : (j + 1) * 128, :] = block
            kt_ref[tile, :, j * 128 : (j + 1) * 128] = block.astype(F32).T.astype(BF16)
        return unused

    lax.fori_loop(0, ks_ref.shape[0], sort, 0)
    apart = lax.broadcasted_iota(jnp.int32, (TILE, 256), 0) - (
        lax.broadcasted_iota(jnp.int32, (TILE, 256), 1) & 127
    )
    for b in range(q_ref.shape[0] // 128):
        own = place[b]
        query = q_ref[b * 128 : (b + 1) * 128, :].astype(F32) * HEAD_DIM**-0.5
        query = heads_across(query, 0).astype(BF16)
        last = own // per

        def step(tile, carry, masked):
            top, summed, acc = carry
            scores = dot(ks_ref[tile], query)
            if masked:
                scores = jnp.where(apart <= own * 128 - tile * TILE, scores, -1e30)
            new_top = jnp.maximum(top, jnp.max(scores, 0, keepdims=True))
            keep = jnp.exp(top - new_top)
            probs = jnp.exp(scores - new_top)
            summed = summed * keep + jnp.sum(probs, 0, keepdims=True)
            acc = acc * keep + dot(kt_ref[tile], probs.astype(BF16))
            return new_top, summed, acc

        carry = (
            jnp.full((1, 256), -1e30, F32),
            jnp.zeros((1, 256), F32),
            jnp.zeros((128, 256), F32),
        )
        carry = lax.fori_loop(0, last, lambda tile, c: step(tile, c, False), carry)
        top, summed, acc = step(last, carry, True)
        result = acc[64:] / summed
        o_ref[b] = result
        lse_ref[b] = top + jnp.log(summed)
        low_ref[b * 128 : (b + 1) * 128, :] = heads_back(result).astype(BF16)


def attend(place, slot, rq, kv_all):
    count = rq.shape[0] // 128
    tiles = kv_all.shape[0] * 128 // TILE
    return pl.pallas_call(
        attend_kernel,
        grid_spec=pltpu.PrefetchScalarGridSpec(
            num_scalar_prefetch=2,
            grid=(1,),
            in_specs=[
                pl.BlockSpec(rq.shape, lambda i, *_: (0, 0)),
                pl.BlockSpec(kv_all.shape, lambda i, *_: (0, 0, 0)),
            ],
            out_specs=[
                pl.BlockSpec(rq.shape, lambda i, *_: (0, 0)),
                pl.BlockSpec((count, 64, 256), lambda i, *_: (0, 0, 0)),
                pl.BlockSpec((count, 1, 256), lambda i, *_: (0, 0, 0)),
                pl.BlockSpec((tiles, TILE, 128), lambda i, *_: (0, 0, 0)),
                pl.BlockSpec((tiles, 128, TILE), lambda i, *_: (0, 0, 0)),
            ],
        ),
        out_shape=[
            jax.ShapeDtypeStruct(rq.shape, BF16),
            jax.ShapeDtypeStruct((count, 64, 256), F32),
            jax.ShapeDtypeStruct((count, 1, 256), F32),
            jax.ShapeDtypeStruct((tiles, TILE, 128), BF16),
            jax.ShapeDtypeStruct((tiles, 128, TILE), BF16),
        ],
        compiler_params=pltpu.CompilerParams(vmem_limit_bytes=LIMIT),
        cost_estimate=pl.CostEstimate(
            flops=20_000_000_000, bytes_accessed=8_000_000, transcendentals=4_000_000
        ),
        name="attend",
    )(place, slot, rq, kv_all)


def attend_back_kernel(
    place, slot, me, q_ref, full_ref, other_ref, o_ref, lse_ref, ks_ref, kt_ref, cos_ref, sin_ref, wo_ref,
    dq_ref, dkv_ref, da_ref, rest_ref, acc_ref,
):
    per = TILE // 128

    def clear(tile, unused):
        acc_ref[tile] = jnp.zeros((TILE, 128), F32)
        return unused

    lax.fori_loop(0, acc_ref.shape[0], clear, 0)
    few, width = full_ref.shape[1], da_ref.shape[1]
    for b in range(full_ref.shape[0]):
        for ref, side in ((full_ref, me[2]), (other_ref, 1 - me[2])):
            at = pl.ds(pl.multiple_of(b * 2 * few + side * few, few), few)
            da_ref[at, :] = ref[b, :, :width]
            rest_ref[at, :] = ref[b, :, width:]
    apart = lax.broadcasted_iota(jnp.int32, (TILE, 256), 0) - (
        lax.broadcasted_iota(jnp.int32, (TILE, 256), 1) & 127
    )
    for b in range(q_ref.shape[0] // 128):
        own = place[b]
        sl = slice(b * 128, (b + 1) * 128)
        query = heads_across(q_ref[sl, :].astype(F32) * HEAD_DIM**-0.5, 0)
        grad = inner(da_ref[sl, :], wo_ref[...]).astype(BF16)
        grad = heads_across(grad.astype(F32), 64)
        delta = jnp.sum(grad[64:] * o_ref[b], 0, keepdims=True)
        lse = lse_ref[b]
        right = jnp.concatenate([query, grad], 1).astype(BF16)
        under = jnp.concatenate([query.T, grad.T], 0).astype(BF16)
        last = own // per

        def step(tile, acc, masked):
            prod = dot(ks_ref[tile], right)
            probs = jnp.exp(prod[:, :256] - lse)
            if masked:
                probs = jnp.where(apart <= own * 128 - tile * TILE, probs, 0.0)
            dscore = (probs * (prod[:, 256:] - delta)).astype(BF16)
            acc_ref[tile] += dot(jnp.concatenate([dscore, probs.astype(BF16)], 1), under)
            return acc + dot(kt_ref[tile], dscore)

        acc = lax.fori_loop(
            0, last, lambda tile, c: step(tile, c, False), jnp.zeros((128, 256), F32)
        )
        acc = step(last, acc, True)
        dq = heads_back(acc[:64]) * HEAD_DIM**-0.5
        dq_ref[sl, :] = full_turn(dq, cos_ref[sl, :], -sin_ref[sl, :]).astype(BF16)

    def unsort(tile, unused):
        for j in range(per):
            dkv_ref[slot[tile * per + j]] = acc_ref[tile, j * 128 : (j + 1) * 128, :].astype(BF16)
        return unused

    lax.fori_loop(0, acc_ref.shape[0], unsort, 0)


def attend_back(place, slot, me, rq, full, other, o, lse, ks, kt, cosine, sine, w_out):
    rows = rq.shape[0]
    width = w_out.shape[1]
    blocks = slot.shape[0]
    args = (rq, full, other, o, lse, ks, kt, cosine, sine)
    shapes = [
        jax.ShapeDtypeStruct(rq.shape, BF16),
        jax.ShapeDtypeStruct((blocks, 128, 128), BF16),
        jax.ShapeDtypeStruct((rows, width), BF16),
        jax.ShapeDtypeStruct((rows, 128), BF16),
    ]
    return pl.pallas_call(
        attend_back_kernel,
        grid_spec=pltpu.PrefetchScalarGridSpec(
            num_scalar_prefetch=3,
            grid=(1,),
            in_specs=[whole(a) for a in args]
            + [pl.BlockSpec((rq.shape[1], width), lambda i, place, slot, me: (me[0], 0))],
            out_specs=[whole(a) for a in shapes],
            scratch_shapes=[pltpu.VMEM(ks.shape, F32)],
        ),
        out_shape=shapes,
        compiler_params=pltpu.CompilerParams(vmem_limit_bytes=LIMIT),
        cost_estimate=pl.CostEstimate(
            flops=30_000_000_000, bytes_accessed=8_000_000, transcendentals=4_000_000
        ),
        name="attend_back",
    )(place, slot, me, *args, w_out)


def whole(a):
    rank = len(a.shape)
    return pl.BlockSpec(a.shape, lambda i, *_: (0,) * rank, pipeline_mode=pl.Buffered(1))


def experts_kernel(
    me, o_ref, p_ref, x_ref, dy_ref, routes_ref, wo0, wo1, wo2, wo3, gain_ref, wr_ref,
    wg_ref, wu_ref, wd_ref,
    x2_ref, h2_ref, mix_ref, keep_ref, give_ref, mkeep_ref, mgive_ref, grad_ref,
    dh2_acc, moe_acc, dmix_acc,
):
    step = pl.program_id(0)
    xh, core, first = me[1], me[2], me[3]
    rows = x_ref.shape[0]
    lane = lax.broadcasted_iota(jnp.int32, (rows, 128), 1)

    @pl.when(step == 0)
    def _():
        def heads(ref, side):
            return jnp.concatenate([ref[side], ref[2 + side]], 1)

        near = dot(heads(o_ref, xh), wo0[...]) + dot(heads(p_ref, xh), wo1[...])
        far = dot(heads(o_ref, 1 - xh), wo2[...]) + dot(heads(p_ref, 1 - xh), wo3[...])
        x2 = x_ref[...].astype(F32) + (near + far)
        x2_ref[...] = x2
        h2 = rms(x2, gain_ref[...])[0].astype(BF16)
        h2_ref[...] = h2
        logits = dot(h2, wr_ref[...])
        routes = routes_ref[...]
        used = lane == routes[:, 0:1]
        for k in range(1, routes.shape[1]):
            used = jnp.logical_or(used, lane == routes[:, k : k + 1])
        top = jnp.max(jnp.where(used, logits, -jnp.inf), 1, keepdims=True)
        expd = jnp.where(used, jnp.exp(logits - top), 0.0)
        mix_ref[...] = expd / jnp.sum(expd, 1, keepdims=True)
        dh2_acc[...] = jnp.zeros_like(dh2_acc)
        moe_acc[...] = jnp.zeros_like(moe_acc)
        dmix_acc[...] = jnp.zeros_like(dmix_acc)

    here = lane == first + step
    gate = jnp.sum(jnp.where(here, mix_ref[...], 0.0), 1, keepdims=True)
    h2 = h2_ref[...]
    dy = dy_ref[...].astype(F32)
    ga = dot(h2, wg_ref[0])
    up = dot(h2, wu_ref[0])
    sig = jax.nn.sigmoid(ga)
    act = ga * sig
    hid = (act * up).astype(BF16)
    eo = dot(hid, wd_ref[0])
    moe_acc[...] += gate * eo
    dmix_acc[...] += jnp.where(here, jnp.sum(dy * eo, 1, keepdims=True), 0.0)
    deo = (gate * dy).astype(BF16)
    dhid = inner(deo, wd_ref[0])
    dga = (dhid * up * (sig * (1.0 + ga * (1.0 - sig)))).astype(BF16)
    dup = (dhid * act).astype(BF16)
    dh2_acc[...] += inner(dga, wg_ref[0]) + inner(dup, wu_ref[0])
    groups = grad_ref.shape[0]
    across = grad_ref.shape[2] * 2 // 3
    width = h2.shape[1]
    grad_ref[:, 0, :across, :512] = outer(h2, dga).astype(BF16).reshape(groups, across, 512)
    grad_ref[:, 0, :across, 512:] = outer(h2, dup).astype(BF16).reshape(groups, across, 512)
    grad_ref[:, 0, across:, :] = outer(hid, deo).astype(BF16).reshape(groups, across // 2, width)

    @pl.when(step == pl.num_programs(0) - 1)
    def _():
        few = rows // 8
        for j in range(4):
            for side, out, mout in ((core, keep_ref, mkeep_ref), (1 - core, give_ref, mgive_ref)):
                at = pl.ds(pl.multiple_of((j * 2 + side) * few, few), few)
                out[j, :, :width] = dh2_acc[at, :].astype(BF16)
                out[j, :, width:] = dmix_acc[at, :].astype(BF16)
                mout[j] = moe_acc[at, :].astype(BF16)


def experts(me, o_mine, o_other, x_pair, dy_pair, routes, wo, gain, router, wg, wu, wd, groups):
    rows, width = x_pair.shape
    few = rows // 8
    local = wg.shape[0] // 2
    ff = wg.shape[2]
    args = (o_mine, o_other, x_pair, dy_pair, routes, *wo, gain, router)
    across = width // groups
    shapes = [
        jax.ShapeDtypeStruct((rows, width), F32),
        jax.ShapeDtypeStruct((rows, width), BF16),
        jax.ShapeDtypeStruct((rows, 128), F32),
        jax.ShapeDtypeStruct((4, few, width + 128), BF16),
        jax.ShapeDtypeStruct((4, few, width + 128), BF16),
        jax.ShapeDtypeStruct((4, few, width), BF16),
        jax.ShapeDtypeStruct((4, few, width), BF16),
    ]
    pick = lambda i, me: (me[0] * local + i, 0, 0)
    return pl.pallas_call(
        experts_kernel,
        grid_spec=pltpu.PrefetchScalarGridSpec(
            num_scalar_prefetch=1,
            grid=(local,),
            in_specs=[whole(a) for a in args]
            + [
                pl.BlockSpec((1, width, ff), pick),
                pl.BlockSpec((1, width, ff), pick),
                pl.BlockSpec((1, ff, width), pick),
            ],
            out_specs=[whole(a) for a in shapes]
            + [pl.BlockSpec((groups, 1, across * 3 // 2, width), lambda i, me: (0, i, 0, 0))],
            scratch_shapes=[
                pltpu.VMEM((rows, width), F32),
                pltpu.VMEM((rows, width), F32),
                pltpu.VMEM((rows, 128), F32),
            ],
        ),
        out_shape=shapes
        + [jax.ShapeDtypeStruct((groups, local, across * 3 // 2, width), BF16)],
        compiler_params=pltpu.CompilerParams(vmem_limit_bytes=56 * 1024 * 1024),
        cost_estimate=pl.CostEstimate(
            flops=20_000_000_000, bytes_accessed=20_000_000, transcendentals=1_000_000
        ),
        name="experts",
    )(me, *args, wg, wu, wd)


def start_kernel(me, x_ref, gain_ref, wq_ref, wk_ref, wv_ref, cos_ref, sin_ref, keep_ref, give_ref):
    h1 = rms(x_ref[...].astype(F32), gain_ref[...])[0].astype(BF16)
    cosine, sine = cos_ref[...], sin_ref[...]
    query = full_turn(dot(h1, wq_ref[...]), cosine, sine)
    key = full_turn(dot(h1, wk_ref[...]), cosine, sine)
    value = dot(h1, wv_ref[...])
    left = lax.broadcasted_iota(jnp.int32, key.shape, 1) < 64
    halves = [
        jnp.concatenate([query[:, :128], jnp.where(left, key, pltpu.roll(value, 64, 1))], 1),
        jnp.concatenate([query[:, 128:], jnp.where(left, pltpu.roll(key, 64, 1), value)], 1),
    ]
    low = me[0] == 0
    keep_ref[...] = jnp.where(low, halves[0], halves[1]).astype(BF16)
    give_ref[...] = jnp.where(low, halves[1], halves[0]).astype(BF16)


def start(me, tokens, gain, wq, wk, wv, cosine, sine):
    args = (tokens, gain, wq, wk, wv, cosine, sine)
    shapes = [jax.ShapeDtypeStruct((tokens.shape[0], 256), BF16)] * 2
    return pl.pallas_call(
        start_kernel,
        grid_spec=pltpu.PrefetchScalarGridSpec(
            num_scalar_prefetch=1,
            grid=(1,),
            in_specs=[whole(a) for a in args],
            out_specs=[whole(a) for a in shapes],
        ),
        out_shape=shapes,
        compiler_params=pltpu.CompilerParams(vmem_limit_bytes=LIMIT),
        name="start",
    )(me, *args)


def middle_kernel(me, part_ref, x2_ref, mix_ref, dy_ref, gain_ref, wr_ref, out_ref):
    part = part_ref[0].astype(F32)
    for j in range(1, part_ref.shape[0]):
        part = part + part_ref[j].astype(F32)
    width = x2_ref.shape[1]
    mix, dmix = mix_ref[...], part[:, width:]
    dlogits = (mix * (dmix - jnp.sum(mix * dmix, 1, keepdims=True))).astype(BF16)
    dh2 = part[:, :width] + inner(dlogits, wr_ref[...])
    x2 = x2_ref[...]
    factor = lax.rsqrt(jnp.mean(x2 * x2, -1, keepdims=True) + EPS)
    scaled = dh2 * gain_ref[...]
    dx2 = dy_ref[...].astype(F32) + (
        factor * scaled - x2 * factor**3 * jnp.mean(scaled * x2, -1, keepdims=True)
    )
    gain = jnp.sum(dh2 * x2 * factor, 0, keepdims=True).astype(BF16).astype(F32)
    rows = x2.shape[0]
    per = width // rows
    at = lax.broadcasted_iota(jnp.int32, (rows, width), 1)
    spread = jnp.where(at // per == lax.broadcasted_iota(jnp.int32, (rows, width), 0), gain, 0.0)
    lane = lax.broadcasted_iota(jnp.int32, (width, 128), 1)
    place = lane == lax.broadcasted_iota(jnp.int32, (width, 128), 0) % per + 16
    extra = dot(spread.astype(BF16), place.astype(F32).astype(BF16)) + dlogits.astype(F32)
    for j in range(out_ref.shape[0]):
        out_ref[j, :, :width] = dx2.astype(BF16)
        out_ref[j, :, width:] = extra.astype(BF16)


def middle(me, part, x2, mix, dy, gain, router):
    few = part.shape[1]
    width = x2.shape[1]
    mine = lambda i, me: (me[4], 0)
    shape = jax.ShapeDtypeStruct(part.shape, BF16)
    return pl.pallas_call(
        middle_kernel,
        grid_spec=pltpu.PrefetchScalarGridSpec(
            num_scalar_prefetch=1,
            grid=(1,),
            in_specs=[
                whole(part),
                pl.BlockSpec((few, width), mine),
                pl.BlockSpec((few, 128), mine),
                pl.BlockSpec((few, width), mine),
                whole(gain),
                whole(router),
            ],
            out_specs=whole(shape),
        ),
        out_shape=shape,
        compiler_params=pltpu.CompilerParams(vmem_limit_bytes=LIMIT),
        name="middle",
    )(me, part, x2, mix, dy, gain, router)


def collect_kernel(part_ref, cos_ref, sin_ref, out_ref):
    total = part_ref[0].astype(F32)
    for j in range(1, part_ref.shape[0]):
        total = total + part_ref[j].astype(F32)
    turned = full_turn(total, cos_ref[...], -sin_ref[...])
    left = lax.broadcasted_iota(jnp.int32, total.shape, 1) < 64
    out_ref[...] = jnp.where(left, turned, total).astype(BF16)


def collect(part, cosine, sine):
    shape = jax.ShapeDtypeStruct(part.shape[1:], BF16)
    args = (part, cosine, sine)
    return pl.pallas_call(
        collect_kernel,
        grid=(1,),
        in_specs=[whole(a) for a in args],
        out_specs=whole(shape),
        out_shape=shape,
        compiler_params=pltpu.CompilerParams(vmem_limit_bytes=LIMIT),
        name="collect",
    )(*args)


def finish_kernel(
    me, qm_ref, qo_ref, km_ref, ko_ref, w0, w1, w2, w3, x_ref, gain_ref, da_ref,
    early_ref, gkv_ref, rest_ref, out_ref, small_ref,
):
    xh = me[1]

    def back(q_ref, kv_ref, side, w):
        left = lax.broadcasted_iota(jnp.int32, kv_ref.shape[1:], 1) < 64
        one, two = kv_ref[side].astype(F32), kv_ref[2 + side].astype(F32)
        keys = jnp.where(left, one, pltpu.roll(two, 64, 1)).astype(BF16)
        values = jnp.where(left, pltpu.roll(one, 64, 1), two).astype(BF16)
        return inner(
            jnp.concatenate([q_ref[side], q_ref[2 + side], keys, values], 1), w[...]
        )

    near = back(qm_ref, km_ref, xh, w0) + back(qo_ref, ko_ref, xh, w1)
    far = back(qm_ref, km_ref, 1 - xh, w2) + back(qo_ref, ko_ref, 1 - xh, w3)
    dh1 = near + far
    x = x_ref[...].astype(F32)
    factor = lax.rsqrt(jnp.mean(x * x, -1, keepdims=True) + EPS)
    scaled = dh1 * gain_ref[...]
    out_ref[...] = (
        da_ref[...].astype(F32)
        + factor * scaled
        - x * factor**3 * jnp.mean(scaled * x, -1, keepdims=True)
    ).astype(BF16)
    gain = jnp.sum(dh1 * x * factor, 0, keepdims=True)
    width = gain.shape[1]
    column = jnp.broadcast_to(gain, (128, width)).T
    lane = lax.broadcasted_iota(jnp.int32, (width, 128), 1)
    mark = rest_ref.shape[1] - 1
    small_ref[:, :256] = early_ref[...]
    small_ref[:, 256:384] = gkv_ref[...]
    small_ref[:, 384:] = jnp.where(lane == mark, column, rest_ref[...].astype(F32)).astype(BF16)


def finish(me, qm, qo, km, ko, ws, tokens, gain, da, early, gkv, rest):
    rows, width = tokens.shape
    args = (qm, qo, km, ko, *ws, tokens, gain)
    shapes = [
        jax.ShapeDtypeStruct((rows, width), BF16),
        jax.ShapeDtypeStruct((width, 512), BF16),
    ]
    return pl.pallas_call(
        finish_kernel,
        grid_spec=pltpu.PrefetchScalarGridSpec(
            num_scalar_prefetch=1,
            grid=(1,),
            in_specs=[whole(a) for a in args]
            + [pl.BlockSpec((rows, width), lambda i, me: (me[0], 0))]
            + [whole(a) for a in (early, gkv, rest)],
            out_specs=[whole(a) for a in shapes],
        ),
        out_shape=shapes,
        compiler_params=pltpu.CompilerParams(vmem_limit_bytes=LIMIT),
        name="finish",
    )(me, *args, da, early, gkv, rest)


def on_device(
    tokens,
    cotangent,
    pairing,
    routes,
    norm_attn,
    w_query,
    w_key,
    w_value,
    w_out,
    norm_moe,
    w_router,
    w_gate,
    w_up,
    w_down,
):
    zy = lax.axis_index(ZY)
    xl = lax.axis_index("xl")
    wa = lax.axis_index(WA)
    rows, width = tokens.shape
    block = rows // 2
    both = 2 * rows
    count_ctx = pairing.shape[0]
    blocks = 2 * count_ctx
    groups = count_ctx // 2
    hq = w_query.shape[1] // 2
    hk = w_key.shape[1] // 2
    hall = hq + 2 * hk

    xh = lax.axis_index("xh")
    core = lax.axis_index("c")
    first = wa * w_gate.shape[0] + xl * (w_gate.shape[0] // 2)
    me = jnp.stack([xl, xh, core, first, xl * 4 + wa]).astype(jnp.int32)

    pair = lax.dynamic_slice_in_dim(pairing, zy * 2, 2)
    starts = jnp.stack([pair, blocks - 1 - pair], 1).reshape(4) * block
    qpos = (starts[:, None] + jnp.arange(block, dtype=jnp.int32)[None, :]).reshape(both)

    cos2, sin2 = lane_angles(qpos)
    own = lambda a: lax.dynamic_slice_in_dim(a, xl * rows, rows, 0)
    keep, give = start(
        me, tokens, norm_attn[None], w_query, w_key, w_value, own(cos2), own(sin2)
    )
    got = lax.ppermute(give, "xl", SWAP)
    low = xl == 0
    qkv = jnp.concatenate([jnp.where(low, keep, got), jnp.where(low, got, keep)], 0)
    rq = qkv[:, :hq]
    kv_mine = qkv[:, hq:]

    kv_all = lax.all_to_all(
        jnp.broadcast_to(kv_mine[None], (groups,) + kv_mine.shape), ZY, 0, 0, tiled=False
    ).reshape(blocks, block, 2 * hk)

    def ring_weights(w):
        near = lax.ppermute(w, "c", SWAP)
        far = lax.ppermute(w, "xh", SWAP)
        return w, near, far, lax.ppermute(far, "c", SWAP)

    w_outs = ring_weights(w_out)
    w_ins = ring_weights(jnp.concatenate([w_query, w_key, w_value], 1))

    def ring_parts(w):
        return w, lax.ppermute(w, "c", SWAP), lax.ppermute(w, "xh", SWAP), lax.ppermute(
            w, WA, [(0, 3), (3, 0), (1, 2), (2, 1)]
        )

    def in_order(parts):
        near = jnp.where(core == 0, jnp.concatenate(parts[:2], 0), jnp.concatenate(parts[1::-1], 0))
        far = jnp.where(core == 0, jnp.concatenate(parts[2:], 0), jnp.concatenate(parts[:1:-1], 0))
        return jnp.where(xh == 0, jnp.concatenate([near, far], 0), jnp.concatenate([far, near], 0))

    x_pair = swap_x(tokens)
    dy_pair = swap_x(cotangent)
    routes_pair = swap_x(routes.astype(F32)).astype(jnp.int32)

    ranks = jnp.arange(count_ctx, dtype=jnp.int32)
    inverse = jnp.sum(jnp.where(pairing[None, :] == ranks[:, None], ranks[None, :], 0), 1)
    slot = jnp.concatenate([inverse * 2, inverse[::-1] * 2 + 1])
    place = starts // block
    attn_low, attn, lse, ks, kt = attend(place, slot, rq, kv_all)

    o_mine = lax.all_to_all(
        jnp.broadcast_to(attn_low[None], (4,) + attn_low.shape), CHIPS, 0, 0, tiled=False
    )
    o_other = lax.ppermute(o_mine, "c", SWAP)
    experts_all = w_router.shape[1]
    router = jnp.pad(w_router, ((0, 0), (0, 128 - experts_all)))
    x2, h2, mix_all, keep, give, mkeep, mgive, grads = experts(
        me, o_mine, o_other, x_pair, dy_pair, routes_pair, w_outs, norm_moe[None], router,
        w_gate, w_up, w_down, groups,
    )

    def add(one, two):
        return (one.astype(F32) + two.astype(F32)).astype(BF16)

    part = add(keep, lax.ppermute(give, "c", SWAP))
    part = lax.all_to_all(part, CHIPS, 0, 0, tiled=False)
    grads = lax.psum_scatter(grads, "z", scatter_dimension=0, tiled=True)
    payload = middle(me, part, x2, mix_all, dy_pair, norm_moe[None], router)
    full = lax.all_to_all(payload, CHIPS, 0, 0, tiled=False)
    other = lax.ppermute(full, "c", SWAP)

    moe = add(mkeep, lax.ppermute(mgive, "c", SWAP))
    moe, full = lax.optimization_barrier((moe, full))
    moe = lax.all_to_all(moe, CHIPS, 0, 0, tiled=False)

    dq, grad_kv, da, rest_pair = attend_back(
        place, slot, me, rq, full, other, attn, lse, ks, kt, cos2, sin2, w_out
    )
    few = both // 8
    mine = lambda a: lax.dynamic_slice_in_dim(a, (xl * 4 + wa) * few, few, 0)
    out_rows = (mine(x2) + jnp.sum(moe.astype(F32), 0)).astype(BF16)
    ones = ring_parts(out_rows)
    output = in_order(ones)
    gnm_all = rest_pair[:, experts_all : experts_all + width // few].astype(F32)
    gnm_own = jnp.sum(own(gnm_all).reshape(4, few, width // few), 0).reshape(width)
    grad_kv = lax.all_to_all(
        grad_kv.reshape(groups, both, 2 * hk), ZY, 0, 0, tiled=False
    )
    grad_kv, grads = lax.optimization_barrier((grad_kv, grads))
    grads = lax.psum_scatter(grads, "y", scatter_dimension=0, tiled=True)[0]
    dkv = collect(grad_kv, cos2, sin2)
    h1 = rms(x_pair.astype(F32), norm_attn)[0].astype(BF16)

    def to_rows(piece):
        n = piece.shape[1]
        parts = piece.reshape(2, rows, n)
        same = lax.dynamic_index_in_dim(parts, xl, 0, False)
        swapped = lax.ppermute(lax.dynamic_index_in_dim(parts, 1 - xl, 0, False), "xl", SWAP)
        both_far = lax.ppermute(jnp.stack([same, swapped]), "xh", SWAP)
        here = jnp.where(low, jnp.stack([same, swapped]), jnp.stack([swapped, same]))
        away = jnp.where(low, both_far, both_far[::-1])
        mine = jnp.where(xh == 0, jnp.stack([here, away], 1), jnp.stack([away, here], 1))
        mine = mine.reshape(4, rows, n)
        return mine, lax.ppermute(mine, "c", SWAP)

    def to_rows_now(piece):
        n = piece.shape[1]
        mine = lax.all_to_all(
            jnp.broadcast_to(piece.reshape(2, 1, rows, n), (2, 2, rows, n)).reshape(4, rows, n),
            CHIPS, 0, 0, tiled=False,
        )
        return mine, lax.ppermute(mine, "c", SWAP)

    dq_mine, dq_other = to_rows(dq)
    kv_mine, kv_other = to_rows_now(dkv)
    h2_own = own(h2)
    rest = jnp.concatenate(
        [outer(h2_own, own(rest_pair)[:, :experts_all]), gnm_own[:, None]], 1
    ).astype(BF16)
    rest = jnp.pad(rest, ((0, 0), (0, 128 - rest.shape[1])))
    early = jnp.concatenate([outer(h1, dq), outer(da, attn_low)], 1).astype(BF16)
    gkv = outer(h1, dkv).astype(BF16)
    grad_tokens, small = finish(
        me, dq_mine, dq_other, kv_mine, kv_other, w_ins, tokens, norm_attn[None], da,
        early, gkv, rest,
    )

    local = grads.shape[0]
    nrow = width // groups // 2
    by_dest = jnp.concatenate(
        [
            grads[:, : 2 * nrow].reshape(local, 2, nrow, width),
            grads[:, 2 * nrow :].reshape(local, 2, nrow // 2, width),
        ],
        2,
    ).transpose(1, 0, 2, 3)
    by_dest, small = lax.optimization_barrier((by_dest, small))
    keep_w = lax.dynamic_index_in_dim(by_dest, xl, 0, False)
    got_w = lax.ppermute(lax.dynamic_index_in_dim(by_dest, 1 - xl, 0, False), "xl", SWAP)

    small = lax.all_to_all(small.reshape(count_ctx, -1, small.shape[1]), CTX, 0, 0, tiled=False)
    small = jnp.sum(small.reshape(groups, 2, -1, small.shape[2]).astype(F32), 0)
    def pair_of(a, n):
        return jnp.concatenate([small[0, :, a : a + n], small[1, :, a : a + n]], 1)

    grad_query = pair_of(0, hq)
    grad_out = pair_of(hq, hq).T
    grad_key = pair_of(2 * hq, hk)
    grad_value = pair_of(2 * hq + hk, hk)
    rest = small[0, :, 3 * hq :] + small[1, :, 3 * hq :]
    grad_router = rest[:, :experts_all]
    grad_norm_moe = rest[:, experts_all]
    grad_norm_attn = rest[:, 127]
    pairw = jnp.concatenate(
        [jnp.where(low, keep_w, got_w), jnp.where(low, got_w, keep_w)], 0
    ).astype(F32)
    half = width // 2
    grad_gate = pairw[:, :nrow, :half]
    grad_up = pairw[:, :nrow, half:]
    grad_down = pairw[:, nrow:]
    return (
        output,
        grad_tokens,
        grad_norm_attn,
        grad_query,
        grad_key,
        grad_value,
        grad_out,
        grad_norm_moe,
        grad_router,
        grad_gate,
        grad_up,
        grad_down,
    )


def solution(mesh):
    fine = Mesh(mesh.devices.reshape(4, 4, 2, 2, 2), ("z", "y", "xl", "xh", "c"))
    return jax.shard_map(
        on_device,
        mesh=fine,
        in_specs=(
            P(CTX, None),
            P(CTX, None),
            P(),
            P(CTX, None),
            P(),
            P(None, WA),
            P(None, WA),
            P(None, WA),
            P(WA, None),
            P(),
            P(),
            P(WA, None, None),
            P(WA, None, None),
            P(WA, None, None),
        ),
        out_specs=(
            P(CTX, None),
            P(CTX, None),
            P(CTX),
            P(CTX, WA),
            P(CTX, WA),
            P(CTX, WA),
            P(WA, CTX),
            P(CTX),
            P(CTX, None),
            P(WA, CTX, None),
            P(WA, CTX, None),
            P(WA, CTX, None),
        ),
        check_vma=False,
    )
```

profile of v0, /device:TPU:1, one launch (start us, length us, event | category | flops | bytes accessed | tf_op | source)
XLA Modules:
  0.0 325.3 jit_solution(10488491996460161344)
XLA Ops:
  15.4 2.1 collective-permute-start
  17.5 2.7 collective-permute-done
  22.1 8.4 %all-to-all-start = ((bf16[16,512,128]{2,1,0:T(8,128)(2,1)}), bf16[16,512,128]{2,1,0:T(8,128)(2,1)}, u32[]{:S(2)}, u32[]{:S(2)}) async-start(bf16[16,512,128]{2,1,0:T(8,128)(2,1)} %broadcast_in_dim.62), calls=%async_computation | async-start | bytes 4194304 | tf_op jit(solution)/shard_map/all_to_all | solution.py:582
  31.8 2.4 collective-permute-start.6
  34.5 23.7 %all-to-all-done = bf16[16,512,128]{2,1,0:T(8,128)(2,1)} async-done(((bf16[16,512,128]{2,1,0:T(8,128)(2,1)}), bf16[16,512,128]{2,1,0:T(8,128)(2,1)}, u32[]{:S(2)}, u32[]{:S(2)}) %all-to-all-start) | async-done | bytes 2097184 | tf_op jit(solution)/shard_map/all_to_all | solution.py:582
  58.2 21.8 %attend.1 = (bf16[512,128]{1,0:T(8,128)(2,1)S(1)}, f32[4,64,256]{2,1,0:T(8,128)S(1)}, f32[4,1,256]{2,1,0:T(1,128)S(1)}, bf16[16,512,128]{2,1,0:T(8,128)(2,1)S(1)}, bf16[16,128,512]{2,1,0:T(8,128)(2,1)S(1)}) custom-call(s32[4]{0:T(128)S(1)} %and_select_fusion.2.place, s32[64]{0:T(128)S(1)} %pad_add_fusion.slot, ...), custom_call_target="tpu_custom_call" | custom-call | flops 20000000000 | bytes 8000000 | tf_op jit(solution)/shard_map/attend/pallas_call | solution.py:127
  84.3 4.1 %all-to-all-start.1 = ((bf16[4,512,128]{2,1,0:T(8,128)(2,1)}), bf16[4,512,128]{2,1,0:T(8,128)(2,1)}, u32[]{:S(2)}, u32[]{:S(2)}) async-start(bf16[4,512,128]{2,1,0:T(8,128)(2,1)} %broadcast_in_dim.63), calls=%async_computation.1 | async-start | bytes 1048576 | tf_op jit(solution)/shard_map/all_to_all | solution.py:614
  90.0 4.7 %collective-permute-start.5 = (bf16[256,1024]{1,0:T(8,128)(2,1)S(1)}, bf16[256,1024]{1,0:T(8,128)(2,1)}, u32[]{:S(2)}, u32[]{:S(2)}) collective-permute-start(bf16[256,1024]{1,0:T(8,128)(2,1)S(1)} %copy-done.29), channel_id=1, source_target_pairs={{0,1},{1,0},{2,3},{3,2},{4,5},{5,4},{6,7},{7,6},{8,9},{9,8},{10,11... | collective-permute-start | bytes 1572872 | tf_op jit(solution)/shard_map/ppermute | solution.py:587
  96.5 5.0 %collective-permute-start.7 = (bf16[256,1024]{1,0:T(8,128)(2,1)}, bf16[256,1024]{1,0:T(8,128)(2,1)}, u32[]{:S(2)}, u32[]{:S(2)}) collective-permute-start(bf16[256,1024]{1,0:T(8,128)(2,1)} %collective-permute-done.6.wo2), channel_id=1, source_target_pairs={{0,1},{1,0},{2,3},{3,2},{4,5},{5,4},{6,7},{7,6},{8,9},{9,8},{10,11... | collective-permute-start | bytes 1572872 | tf_op jit(solution)/shard_map/ppermute | solution.py:589
  102.9 5.9 %collective-permute-done.3 = bf16[256,1024]{1,0:T(8,128)(2,1)} collective-permute-done((bf16[256,1024]{1,0:T(8,128)(2,1)S(1)}, bf16[256,1024]{1,0:T(8,128)(2,1)}, u32[]{:S(2)}, u32[]{:S(2)}) %collective-permute-start.3) | collective-permute-done | bytes 524320 | tf_op jit(solution)/shard_map/ppermute | solution.py:39
  112.4 22.0 %experts.1 = (f32[512,1024]{1,0:T(8,128)}, bf16[512,1024]{1,0:T(8,128)(2,1)}, f32[512,128]{1,0:T(8,128)}, bf16[4,64,1152]{2,1,0:T(8,128)(2,1)}, bf16[4,64,1152]{...) custom-call(s32[5]{0:T(128)} %copy-done.26, ...), custom_call_target="tpu_custom_call" | custom-call | flops 20000000000 | bytes 20000000 | tf_op jit(solution)/shard_map/experts/pallas_call | solution.py:336
  139.4 12.8 %all_to_all.40.part_ref = bf16[4,64,1152]{2,1,0:T(8,128)(2,1)S(1)} all-to-all(bf16[4,64,1152]{2,1,0:T(8,128)(2,1)S(1)} %add_convert_fusion), channel_id=1, replica_groups=mesh['z'=4,'y'=4,'xl'=2,'xh'=2,'c'=2] {'xl','xh'}, dimensions={0} | all-to-all | bytes 1179648 | tf_op jit(solution)/shard_map/all_to_all | solution.py:629
  154.2 3.6 %all-to-all-start.3 = ((bf16[4,64,1152]{2,1,0:T(8,128)(2,1)}), bf16[4,64,1152]{2,1,0:T(8,128)(2,1)S(1)}, u32[]{:S(2)}, u32[]{:S(2)}) async-start(bf16[4,64,1152]{2,1,0:T(8,128)(2,1)} %middle.1), calls=%async_computation.3 | async-start | bytes 1179648 | tf_op jit(solution)/shard_map/all_to_all | solution.py:632
  159.5 8.3 %all-to-all-done.3.full_ref = bf16[4,64,1152]{2,1,0:T(8,128)(2,1)S(1)} async-done(((bf16[4,64,1152]{2,1,0:T(8,128)(2,1)}), bf16[4,64,1152]{2,1,0:T(8,128)(2,1)S(1)}, u32[]{:S(2)}, u32[]{:S(2)}) %all-to-all-start.3) | async-done | bytes 589856 | tf_op jit(solution)/shard_map/all_to_all | solution.py:632
  170.7 22.2 %attend_back.1 = (bf16[512,128]{1,0:T(8,128)(2,1)S(1)}, bf16[64,128,128]{2,1,0:T(8,128)(2,1)S(1)}, bf16[512,1024]{1,0:T(8,128)(2,1)S(1)}, bf16[512,128]{1,0:T(8,128)(2,1)S(1)}) custom-call(s32[4]{0:T(128)S(1)} %and_select_fusion.2.place, s32[64]{0:T(128)S(1)} %pad_add_fusion.slot, s32[5]{0:T(128)S(1)} %copy-done.27, ...), custom_call_target="tpu_custom_call" | custom-call | flops 30000001024 | bytes 8000000 | tf_op jit(solution)/shard_map/attend_back/pallas_call | solution.py:226
  196.5 4.4 %all-to-all-start.5 = ((bf16[16,512,128]{2,1,0:T(8,128)(2,1)}), bf16[16,512,128]{2,1,0:T(8,128)(2,1)S(1)}, u32[]{:S(2)}, u32[]{:S(2)}) async-start(bf16[16,512,128]{2,1,0:T(8,128)(2,1)} %bitcast.65), calls=%async_computation.5 | async-start | bytes 4194304 | tf_op jit(solution)/shard_map/all_to_all | solution.py:649
  206.4 27.7 %all-to-all-done.5.part_ref = bf16[16,512,128]{2,1,0:T(8,128)(2,1)S(1)} async-done(((bf16[16,512,128]{2,1,0:T(8,128)(2,1)}), bf16[16,512,128]{2,1,0:T(8,128)(2,1)S(1)}, u32[]{:S(2)}, u32[]{:S(2)}) %all-to-all-start.5) | async-done | bytes 2097184 | tf_op jit(solution)/shard_map/all_to_all | solution.py:649
  234.2 4.3 %all-to-all-start.4 = ((bf16[4,64,1024]{2,1,0:T(8,128)(2,1)}), bf16[4,64,1024]{2,1,0:T(8,128)(2,1)}, u32[]{:S(2)}, u32[]{:S(2)}) async-start(bf16[4,64,1024]{2,1,0:T(8,128)(2,1)} %add_convert_fusion.1), calls=%async_computation.4 | async-start | bytes 1048576 | tf_op jit(solution)/shard_map/all_to_all | solution.py:637
  241.4 6.4 %all-to-all-done.4 = bf16[4,64,1024]{2,1,0:T(8,128)(2,1)} async-done(((bf16[4,64,1024]{2,1,0:T(8,128)(2,1)}), bf16[4,64,1024]{2,1,0:T(8,128)(2,1)}, u32[]{:S(2)}, u32[]{:S(2)}) %all-to-all-start.4) | async-done | bytes 524320 | tf_op jit(solution)/shard_map/all_to_all | solution.py:637
  263.5 3.4 %all-to-all-start.6 = ((bf16[4,256,128]{2,1,0:T(8,128)(2,1)}), bf16[4,256,128]{2,1,0:T(8,128)(2,1)S(1)}, u32[]{:S(2)}, u32[]{:S(2)}) async-start(bf16[4,256,128]{2,1,0:T(8,128)(2,1)} %bitcast.20), calls=%async_computation.7 | async-start | bytes 524288 | tf_op jit(solution)/shard_map/all_to_all | solution.py:671
  272.1 2.1 collective-permute-start.17
  284.1 5.6 %finish.1 = (bf16[256,1024]{1,0:T(8,128)(2,1)}, bf16[1024,512]{1,0:T(8,128)(2,1)}) custom-call(s32[5]{0:T(128)S(1)} %copy-done.27, bf16[4,256,128]{2,1,0:T(8,128)(2,1)S(1)} %bitcast.67, bf16[4,256,128]{2,1,0:T(8,128)(2,1)S(1)} %copy-done.18, bf16[4,256,128]{2,1,0:T(8,128)(2,1)S(1)} %all-to-all-done.6.km_ref, bf16[4,256,128]{2,1,0:T(8,128)(2,1)S(1)} %copy-done.20, ...), custom_call_target="tpu_custom_call" | custom-call | tf_op jit(solution)/shard_map/finish/pallas_call | solution.py:517
  291.7 3.9 %all-to-all-start.7 = ((bf16[32,32,512]{2,1,0:T(8,128)(2,1)}), bf16[32,32,512]{2,1,0:T(8,128)(2,1)S(1)}, u32[]{:S(2)}, u32[]{:S(2)}) async-start(bf16[32,32,512]{2,1,0:T(8,128)(2,1)} %bitcast.26), calls=%async_computation.9 | async-start | bytes 2097152 | tf_op jit(solution)/shard_map/all_to_all | solution.py:704
  300.0 12.6 %collective-permute-done.21 = bf16[2,48,1024]{2,1,0:T(8,128)(2,1)S(1)} collective-permute-done((bf16[2,48,1024]{2,1,0:T(8,128)(2,1)S(1)}, bf16[2,48,1024]{2,1,0:T(8,128)(2,1)S(1)}, u32[]{:S(2)}, u32[]{:S(2)}) %collective-permute-start.21) | collective-permute-done | bytes 196640 | tf_op jit(solution)/shard_map/ppermute | solution.py:702
  (217 shorter events, 90.4 us)
Async XLA Ops:
  22.1 36.1 %all-to-all-start = ((bf16[16,512,128]{2,1,0:T(8,128)(2,1)}), bf16[16,512,128]{2,1,0:T(8,128)(2,1)}, u32[]{:S(2)}, u32[]{:S(2)}) async-start(bf16[16,512,128]{2,1,0:T(8,128)(2,1)} %broadcast_in_dim.62), calls=%async_computation | async-start | bytes 4194304 | tf_op jit(solution)/shard_map/all_to_all | solution.py:582
  30.5 71.3 %collective-permute-start.2 = (bf16[256,1024]{1,0:T(8,128)(2,1)S(1)}, bf16[256,1024]{1,0:T(8,128)(2,1)}, u32[]{:S(2)}, u32[]{:S(2)}) collective-permute-start(bf16[256,1024]{1,0:T(8,128)(2,1)S(1)} %copy-done.1), channel_id=1, source_target_pairs={{0,4},{4,0},{1,5},{5,1},{2,6},{6,2},{3,7},{7,3},{8,12},{12,8},{9,1... | collective-permute-start | bytes 1572872 | tf_op jit(solution)/shard_map/ppermute | solution.py:39
  31.8 64.7 %collective-permute-start.6 = (bf16[256,1024]{1,0:T(8,128)(2,1)S(1)}, bf16[256,1024]{1,0:T(8,128)(2,1)}, u32[]{:S(2)}, u32[]{:S(2)}) collective-permute-start(bf16[256,1024]{1,0:T(8,128)(2,1)S(1)} %copy-done.29), channel_id=1, source_target_pairs={{0,2},{2,0},{1,3},{3,1},{4,6},{6,4},{5,7},{7,5},{8,10},{10,8},{9,1... | collective-permute-start | bytes 1572872 | tf_op jit(solution)/shard_map/ppermute | solution.py:588
  84.3 17.2 %all-to-all-start.1 = ((bf16[4,512,128]{2,1,0:T(8,128)(2,1)}), bf16[4,512,128]{2,1,0:T(8,128)(2,1)}, u32[]{:S(2)}, u32[]{:S(2)}) async-start(bf16[4,512,128]{2,1,0:T(8,128)(2,1)} %broadcast_in_dim.63), calls=%async_computation.1 | async-start | bytes 1048576 | tf_op jit(solution)/shard_map/all_to_all | solution.py:614
  88.5 145.6 %reduce-scatter.3.cloned.1.call-start = ((), (), s32[]{:S(2)}) async-start(), calls=%async_computation.10 | async-start | bytes 7864320 | tf_op jit(solution)/shard_map/reduce_scatter | solution.py:630
  90.0 21.6 %collective-permute-start.5 = (bf16[256,1024]{1,0:T(8,128)(2,1)S(1)}, bf16[256,1024]{1,0:T(8,128)(2,1)}, u32[]{:S(2)}, u32[]{:S(2)}) collective-permute-start(bf16[256,1024]{1,0:T(8,128)(2,1)S(1)} %copy-done.29), channel_id=1, source_target_pairs={{0,1},{1,0},{2,3},{3,2},{4,5},{5,4},{6,7},{7,6},{8,9},{9,8},{10,11... | collective-permute-start | bytes 1572872 | tf_op jit(solution)/shard_map/ppermute | solution.py:587
  94.7 14.1 %collective-permute-start.3 = (bf16[256,1024]{1,0:T(8,128)(2,1)S(1)}, bf16[256,1024]{1,0:T(8,128)(2,1)}, u32[]{:S(2)}, u32[]{:S(2)}) collective-permute-start(bf16[256,1024]{1,0:T(8,128)(2,1)S(1)} %copy-done.40), channel_id=1, source_target_pairs={{0,4},{4,0},{1,5},{5,1},{2,6},{6,2},{3,7},{7,3},{8,12},{12,8},{9,1... | collective-permute-start | bytes 1572872 | tf_op jit(solution)/shard_map/ppermute | solution.py:39
  96.5 15.1 %collective-permute-start.7 = (bf16[256,1024]{1,0:T(8,128)(2,1)}, bf16[256,1024]{1,0:T(8,128)(2,1)}, u32[]{:S(2)}, u32[]{:S(2)}) collective-permute-start(bf16[256,1024]{1,0:T(8,128)(2,1)} %collective-permute-done.6.wo2), channel_id=1, source_target_pairs={{0,1},{1,0},{2,3},{3,2},{4,5},{5,4},{6,7},{7,6},{8,9},{9,8},{10,11... | collective-permute-start | bytes 1572872 | tf_op jit(solution)/shard_map/ppermute | solution.py:589
  101.5 10.1 %collective-permute-start.1 = (bf16[4,512,128]{2,1,0:T(8,128)(2,1)}, bf16[4,512,128]{2,1,0:T(8,128)(2,1)S(1)}, u32[]{:S(2)}, u32[]{:S(2)}) collective-permute-start(bf16[4,512,128]{2,1,0:T(8,128)(2,1)} %all-to-all-done.1.o_ref), channel_id=1, source_target_pairs={{0,1},{1,0},{2,3},{3,2},{4,5},{5,4},{6,7},{7,6},{8,9},{9,8},{10,11... | collective-permute-start | bytes 1572872 | tf_op jit(solution)/shard_map/ppermute | solution.py:617
  154.2 13.6 %all-to-all-start.3 = ((bf16[4,64,1152]{2,1,0:T(8,128)(2,1)}), bf16[4,64,1152]{2,1,0:T(8,128)(2,1)S(1)}, u32[]{:S(2)}, u32[]{:S(2)}) async-start(bf16[4,64,1152]{2,1,0:T(8,128)(2,1)} %middle.1), calls=%async_computation.3 | async-start | bytes 1179648 | tf_op jit(solution)/shard_map/all_to_all | solution.py:632
  157.8 10.8 %collective-permute-start.8 = (bf16[4,64,1024]{2,1,0:T(8,128)(2,1)}, bf16[4,64,1024]{2,1,0:T(8,128)(2,1)S(1)}, u32[]{:S(2)}, u32[]{:S(2)}) collective-permute-start(bf16[4,64,1024]{2,1,0:T(8,128)(2,1)} %get-tuple-element.44), channel_id=1, source_target_pairs={{0,1},{1,0},{2,3},{3,2},{4,5},{5,4},{6,7},{7,6},{8,9},{9,8},{10,11... | collective-permute-start | bytes 1572872 | tf_op jit(solution)/shard_map/ppermute | solution.py:635
  196.5 37.6 %all-to-all-start.5 = ((bf16[16,512,128]{2,1,0:T(8,128)(2,1)}), bf16[16,512,128]{2,1,0:T(8,128)(2,1)S(1)}, u32[]{:S(2)}, u32[]{:S(2)}) async-start(bf16[16,512,128]{2,1,0:T(8,128)(2,1)} %bitcast.65), calls=%async_computation.5 | async-start | bytes 4194304 | tf_op jit(solution)/shard_map/all_to_all | solution.py:649
  200.9 88.9 %reduce-scatter.5.cloned.1.call-start = ((), (), s32[]{:S(2)}) async-start(), calls=%async_computation.11 | async-start | bytes 1966080 | tf_op jit(solution)/shard_map/reduce_scatter | solution.py:653
  205.1 36.2 %collective-permute-start.19 = (bf16[1024,512]{1,0:T(8,128)(2,1)}, bf16[1024,512]{1,0:T(8,128)(2,1)}, u32[]{:S(2)}, u32[]{:S(2)}) collective-permute-start(bf16[1024,512]{1,0:T(8,128)(2,1)} %constant_dynamic-update-slice_fusion.w0), channel_id=1, source_target_pairs={{0,2},{2,0},{1,3},{3,1},{4,6},{6,4},{5,7},{7,5},{8,10},{10,8},{9,1... | collective-permute-start | bytes 3145736 | tf_op jit(solution)/shard_map/ppermute | solution.py:588
  234.2 13.6 %all-to-all-start.4 = ((bf16[4,64,1024]{2,1,0:T(8,128)(2,1)}), bf16[4,64,1024]{2,1,0:T(8,128)(2,1)}, u32[]{:S(2)}, u32[]{:S(2)}) async-start(bf16[4,64,1024]{2,1,0:T(8,128)(2,1)} %add_convert_fusion.1), calls=%async_computation.4 | async-start | bytes 1048576 | tf_op jit(solution)/shard_map/all_to_all | solution.py:637
  238.5 39.1 %collective-permute-start.18 = (bf16[1024,512]{1,0:T(8,128)(2,1)}, bf16[1024,512]{1,0:T(8,128)(2,1)}, u32[]{:S(2)}, u32[]{:S(2)}) collective-permute-start(bf16[1024,512]{1,0:T(8,128)(2,1)} %constant_dynamic-update-slice_fusion.w0), channel_id=1, source_target_pairs={{0,1},{1,0},{2,3},{3,2},{4,5},{5,4},{6,7},{7,6},{8,9},{9,8},{10,11... | collective-permute-start | bytes 3145736 | tf_op jit(solution)/shard_map/ppermute | solution.py:587
  241.3 37.5 %collective-permute-start.20 = (bf16[1024,512]{1,0:T(8,128)(2,1)}, bf16[1024,512]{1,0:T(8,128)(2,1)}, u32[]{:S(2)}, u32[]{:S(2)}) collective-permute-start(bf16[1024,512]{1,0:T(8,128)(2,1)} %collective-permute-done.19.w2), channel_id=1, source_target_pairs={{0,1},{1,0},{2,3},{3,2},{4,5},{5,4},{6,7},{7,6},{8,9},{9,8},{10,11... | collective-permute-start | bytes 3145736 | tf_op jit(solution)/shard_map/ppermute | solution.py:589
  250.7 44.9 %collective-permute-start.10 = (bf16[64,1024]{1,0:T(8,128)(2,1)}, bf16[64,1024]{1,0:T(8,128)(2,1)}, u32[]{:S(2)}, u32[]{:S(2)}) collective-permute-start(bf16[64,1024]{1,0:T(8,128)(2,1)} %add_convert_fusion.2), channel_id=1, source_target_pairs={{0,1},{1,0},{2,3},{3,2},{4,5},{5,4},{6,7},{7,6},{8,9},{9,8},{10,11... | collective-permute-start | bytes 393224 | tf_op jit(solution)/shard_map/ppermute | solution.py:595
  256.2 10.7 %collective-permute-start.15 = (bf16[2,256,128]{2,1,0:T(8,128)(2,1)}, bf16[2,256,128]{2,1,0:T(8,128)(2,1)}, u32[]{:S(2)}, u32[]{:S(2)}) collective-permute-start(bf16[2,256,128]{2,1,0:T(8,128)(2,1)} %pad_maximum_fusion.4), channel_id=1, source_target_pairs={{0,2},{2,0},{1,3},{3,1},{4,6},{6,4},{5,7},{7,5},{8,10},{10,8},{9,1... | collective-permute-start | bytes 393224 | tf_op jit(solution)/shard_map/ppermute | solution.py:662
  269.0 11.8 %collective-permute-start.16 = (bf16[4,256,128]{2,1,0:T(8,128)(2,1)S(1)}, bf16[4,256,128]{2,1,0:T(8,128)(2,1)S(1)}, u32[]{:S(2)}, u32[]{:S(2)}) collective-permute-start(bf16[4,256,128]{2,1,0:T(8,128)(2,1)S(1)} %bitcast.66), channel_id=1, source_target_pairs={{0,1},{1,0},{2,3},{3,2},{4,5},{5,4},{6,7},{7,6},{8,9},{9,8},{10,11... | collective-permute-start | bytes 786440 | tf_op jit(solution)/shard_map/ppermute | solution.py:667
  277.6 20.4 %collective-permute-start.11 = (bf16[64,1024]{1,0:T(8,128)(2,1)}, bf16[64,1024]{1,0:T(8,128)(2,1)S(1)}, u32[]{:S(2)}, u32[]{:S(2)}) collective-permute-start(bf16[64,1024]{1,0:T(8,128)(2,1)} %add_convert_fusion.2), channel_id=1, source_target_pairs={{0,2},{2,0},{1,3},{3,1},{4,6},{6,4},{5,7},{7,5},{8,10},{10,8},{9,1... | collective-permute-start | bytes 393224 | tf_op jit(solution)/shard_map/ppermute | solution.py:595
  278.9 19.2 %collective-permute-start.12 = (bf16[64,1024]{1,0:T(8,128)(2,1)}, bf16[64,1024]{1,0:T(8,128)(2,1)}, u32[]{:S(2)}, u32[]{:S(2)}) collective-permute-start(bf16[64,1024]{1,0:T(8,128)(2,1)} %add_convert_fusion.2), channel_id=1, source_target_pairs={{0,3},{3,0},{1,2},{2,1},{4,7},{7,4},{5,6},{6,5},{8,11},{11,8},{9,1... | collective-permute-start | bytes 393224 | tf_op jit(solution)/shard_map/ppermute | solution.py:595
  291.7 22.6 %all-to-all-start.7 = ((bf16[32,32,512]{2,1,0:T(8,128)(2,1)}), bf16[32,32,512]{2,1,0:T(8,128)(2,1)S(1)}, u32[]{:S(2)}, u32[]{:S(2)}) async-start(bf16[32,32,512]{2,1,0:T(8,128)(2,1)} %bitcast.26), calls=%async_computation.9 | async-start | bytes 2097152 | tf_op jit(solution)/shard_map/all_to_all | solution.py:704
  296.8 15.8 %collective-permute-start.21 = (bf16[2,48,1024]{2,1,0:T(8,128)(2,1)S(1)}, bf16[2,48,1024]{2,1,0:T(8,128)(2,1)S(1)}, u32[]{:S(2)}, u32[]{:S(2)}) collective-permute-start(bf16[2,48,1024]{2,1,0:T(8,128)(2,1)S(1)} %dynamic-slice_bitcast_fusion), channel_id=1, source_target_pairs={{0,4},{4,0},{1,5},{5,1},{2,6},{6,2},{3,7},{7,3},{8,12},{12,8},{9,1... | collective-permute-start | bytes 589832 | tf_op jit(solution)/shard_map/ppermute | solution.py:702
  (54 other events, 626.8 us)
Sparse Core Ops, SparseCore 0:
  134.6 63.9 reduce-scatter.2
  234.3 21.7 reduce-scatter.4
where the time goes:
time: 327 us; the launch traced here: 325 us
  waiting for transfers between devices  92.6 us (28%)
  Pallas kernels  75.2 us (23%)
  starting transfers between devices  66.2 us (20%)
  local copies, waits for them, and re-layouts  34.4 us (11%)
  other arithmetic  25.6 us (8%)
  between operations  14.7 us (4%)
  blocking collectives  12.8 us (4%)
  matrix products  3.83 us (1%)
    all_to_all x1, waiting for transfers between devices, on_device(): lax.all_to_all(grad_kv.reshape(groups, both, 2 * hk), ZY, 0, 0, tiled=False)  27.7 us
    all_to_all x1, waiting for transfers between devices, on_device(): lax.all_to_all(jnp.broadcast_to(kv_mine[None], (groups,) + kv_mine.shape)...  23.7 us
    pallas_call x1, Pallas kernels, attend_back(): pl.pallas_call(attend_back_kernel, grid_spec=pltpu.PrefetchScalarGridSpec...  22.2 us
    pallas_call x1, Pallas kernels, experts(): pl.pallas_call(experts_kernel, grid_spec=pltpu.PrefetchScalarGridSpec(num...  22 us
    pallas_call x1, Pallas kernels, attend(): pl.pallas_call(attend_kernel, grid_spec=pltpu.PrefetchScalarGridSpec(num_...  21.8 us
    unnamed x98, local copies, waits for them, and re-layouts  20.3 us
    all_to_all x1, blocking collectives, on_device(): part = lax.all_to_all(part, CHIPS, 0, 0, tiled=False)  12.8 us
    ppermute x1, waiting for transfers between devices, on_device(): lax.ppermute(lax.dynamic_index_in_dim(by_dest, 1 - xl, 0, False), 'xl', S...  12.6 us
  transfers between devices with their start and end apart: 31, of which 10 were waited for; matrix products, arithmetic and copies ran while one was open for 12% of the time, Pallas kernels for 16%

commit v1 on v0

--- a/solution.py
+++ b/solution.py
@@ -41,7 +41,7 @@
     return jnp.concatenate([jnp.where(low, mine, other), jnp.where(low, other, mine)], 0)
 
 
-TILE = 512
+TILE = 1024
 LIMIT = 48 * 1024 * 1024
 
 
@@ -76,7 +76,21 @@
     return jnp.concatenate([both[:, :128], both[:, 128:]], 0).T
 
 
-def attend_kernel(place, slot, q_ref, kv_ref, low_ref, o_ref, lse_ref, ks_ref, kt_ref):
+def turns(place, step, per):
+    for pair in (0, 1):
+        late = place[2 * pair + 1]
+        count = late // per + 1
+        first = step < count
+        yield (
+            jnp.where(first, 2 * pair + 1, 2 * pair),
+            jnp.where(first, step, step - count),
+            jnp.where(first, late, place[2 * pair]),
+        )
+
+
+def attend_kernel(
+    place, slot, q_ref, kv_ref, low_ref, o_ref, lse_ref, ks_ref, kt_ref, query_s, top_s, sum_s, acc_s
+):
     per = TILE // 128
 
     def sort(tile, unused):
@@ -90,34 +104,35 @@
     apart = lax.broadcasted_iota(jnp.int32, (TILE, 256), 0) - (
         lax.broadcasted_iota(jnp.int32, (TILE, 256), 1) & 127
     )
-    for b in range(q_ref.shape[0] // 128):
-        own = place[b]
+    count = q_ref.shape[0] // 128
+    for b in range(count):
         query = q_ref[b * 128 : (b + 1) * 128, :].astype(F32) * HEAD_DIM**-0.5
-        query = heads_across(query, 0).astype(BF16)
-        last = own // per
-
-        def step(tile, carry, masked):
-            top, summed, acc = carry
-            scores = dot(ks_ref[tile], query)
-            if masked:
-                scores = jnp.where(apart <= own * 128 - tile * TILE, scores, -1e30)
-            new_top = jnp.maximum(top, jnp.max(scores, 0, keepdims=True))
+        query_s[b] = heads_across(query, 0).astype(BF16)
+    top_s[...] = jnp.full(top_s.shape, -1e30, F32)
+    sum_s[...] = jnp.zeros(sum_s.shape, F32)
+    acc_s[...] = jnp.zeros(acc_s.shape, F32)
+
+    def step(index, unused):
+        work = list(turns(place, index, per))
+        scores = [
+            jnp.where(apart <= own * 128 - tile * TILE, dot(ks_ref[tile], query_s[b]), -1e30)
+            for b, tile, own in work
+        ]
+        for (b, tile, own), score in zip(work, scores):
+            top = top_s[b]
+            new_top = jnp.maximum(top, jnp.max(score, 0, keepdims=True))
             keep = jnp.exp(top - new_top)
-            probs = jnp.exp(scores - new_top)
-            summed = summed * keep + jnp.sum(probs, 0, keepdims=True)
-            acc = acc * keep + dot(kt_ref[tile], probs.astype(BF16))
-            return new_top, summed, acc
-
-        carry = (
-            jnp.full((1, 256), -1e30, F32),
-            jnp.zeros((1, 256), F32),
-            jnp.zeros((128, 256), F32),
-        )
-        carry = lax.fori_loop(0, last, lambda tile, c: step(tile, c, False), carry)
-        top, summed, acc = step(last, carry, True)
-        result = acc[64:] / summed
+            probs = jnp.exp(score - new_top)
+            top_s[b] = new_top
+            sum_s[b] = sum_s[b] * keep + jnp.sum(probs, 0, keepdims=True)
+            acc_s[b] = acc_s[b] * keep + dot(kt_ref[tile], probs.astype(BF16))
+        return unused
+
+    lax.fori_loop(0, ks_ref.shape[0] + 1, step, 0, unroll=3)
+    for b in range(count):
+        result = acc_s[b][64:] / sum_s[b]
         o_ref[b] = result
-        lse_ref[b] = top + jnp.log(summed)
+        lse_ref[b] = top_s[b] + jnp.log(sum_s[b])
         low_ref[b * 128 : (b + 1) * 128, :] = heads_back(result).astype(BF16)
 
 
@@ -140,6 +155,12 @@
                 pl.BlockSpec((tiles, TILE, 128), lambda i, *_: (0, 0, 0)),
                 pl.BlockSpec((tiles, 128, TILE), lambda i, *_: (0, 0, 0)),
             ],
+            scratch_shapes=[
+                pltpu.VMEM((count, 128, 256), BF16),
+                pltpu.VMEM((count, 1, 256), F32),
+                pltpu.VMEM((count, 1, 256), F32),
+                pltpu.VMEM((count, 128, 256), F32),
+            ],
         ),
         out_shape=[
             jax.ShapeDtypeStruct(rq.shape, BF16),
@@ -158,7 +179,7 @@
 
 def attend_back_kernel(
     place, slot, me, q_ref, full_ref, other_ref, o_ref, lse_ref, ks_ref, kt_ref, cos_ref, sin_ref, wo_ref,
-    dq_ref, dkv_ref, da_ref, rest_ref, acc_ref,
+    dq_ref, dkv_ref, da_ref, rest_ref, acc_ref, right_s, under_s, delta_s, dq_s,
 ):
     per = TILE // 128
 
@@ -176,32 +197,35 @@
     apart = lax.broadcasted_iota(jnp.int32, (TILE, 256), 0) - (
         lax.broadcasted_iota(jnp.int32, (TILE, 256), 1) & 127
     )
-    for b in range(q_ref.shape[0] // 128):
-        own = place[b]
+    count = q_ref.shape[0] // 128
+    for b in range(count):
         sl = slice(b * 128, (b + 1) * 128)
         query = heads_across(q_ref[sl, :].astype(F32) * HEAD_DIM**-0.5, 0)
         grad = inner(da_ref[sl, :], wo_ref[...]).astype(BF16)
         grad = heads_across(grad.astype(F32), 64)
-        delta = jnp.sum(grad[64:] * o_ref[b], 0, keepdims=True)
-        lse = lse_ref[b]
-        right = jnp.concatenate([query, grad], 1).astype(BF16)
-        under = jnp.concatenate([query.T, grad.T], 0).astype(BF16)
-        last = own // per
-
-        def step(tile, acc, masked):
-            prod = dot(ks_ref[tile], right)
-            probs = jnp.exp(prod[:, :256] - lse)
-            if masked:
-                probs = jnp.where(apart <= own * 128 - tile * TILE, probs, 0.0)
-            dscore = (probs * (prod[:, 256:] - delta)).astype(BF16)
-            acc_ref[tile] += dot(jnp.concatenate([dscore, probs.astype(BF16)], 1), under)
-            return acc + dot(kt_ref[tile], dscore)
-
-        acc = lax.fori_loop(
-            0, last, lambda tile, c: step(tile, c, False), jnp.zeros((128, 256), F32)
-        )
-        acc = step(last, acc, True)
-        dq = heads_back(acc[:64]) * HEAD_DIM**-0.5
+        delta_s[b] = jnp.sum(grad[64:] * o_ref[b], 0, keepdims=True)
+        right_s[b] = jnp.concatenate([query, grad], 1).astype(BF16)
+        under_s[b] = jnp.concatenate([query.T, grad.T], 0).astype(BF16)
+    dq_s[...] = jnp.zeros(dq_s.shape, F32)
+
+    def step(index, unused):
+        work = list(turns(place, index, per))
+        prods = [dot(ks_ref[tile], right_s[b]) for b, tile, own in work]
+        sides = []
+        for (b, tile, own), prod in zip(work, prods):
+            probs = jnp.exp(prod[:, :256] - lse_ref[b])
+            probs = jnp.where(apart <= own * 128 - tile * TILE, probs, 0.0)
+            dscore = (probs * (prod[:, 256:] - delta_s[b])).astype(BF16)
+            sides.append(jnp.concatenate([dscore, probs.astype(BF16)], 1))
+        for (b, tile, own), side in zip(work, sides):
+            acc_ref[tile] += dot(side, under_s[b])
+            dq_s[b] += dot(kt_ref[tile], side[:, :256])
+        return unused
+
+    lax.fori_loop(0, ks_ref.shape[0] + 1, step, 0, unroll=3)
+    for b in range(count):
+        sl = slice(b * 128, (b + 1) * 128)
+        dq = heads_back(dq_s[b][:64]) * HEAD_DIM**-0.5
         dq_ref[sl, :] = full_turn(dq, cos_ref[sl, :], -sin_ref[sl, :]).astype(BF16)
 
     def unsort(tile, unused):
@@ -231,7 +255,13 @@
             in_specs=[whole(a) for a in args]
             + [pl.BlockSpec((rq.shape[1], width), lambda i, place, slot, me: (me[0], 0))],
             out_specs=[whole(a) for a in shapes],
-            scratch_shapes=[pltpu.VMEM(ks.shape, F32)],
+            scratch_shapes=[
+                pltpu.VMEM(ks.shape, F32),
+                pltpu.VMEM((rows // 128, 128, 512), BF16),
+                pltpu.VMEM((rows // 128, 512, 128), BF16),
+                pltpu.VMEM((rows // 128, 1, 256), F32),
+                pltpu.VMEM((rows // 128, 128, 256), F32),
+            ],
         ),
         out_shape=shapes,
         compiler_params=pltpu.CompilerParams(vmem_limit_bytes=LIMIT),
@@ -390,7 +420,7 @@
             out_specs=[whole(a) for a in shapes],
         ),
         out_shape=shapes,
-        compiler_params=pltpu.CompilerParams(vmem_limit_bytes=LIMIT),
+        compiler_params=pltpu.CompilerParams(vmem_limit_bytes=60 * 1024 * 1024),
         name="start",
     )(me, *args)
 
@@ -443,7 +473,7 @@
             out_specs=whole(shape),
         ),
         out_shape=shape,
-        compiler_params=pltpu.CompilerParams(vmem_limit_bytes=LIMIT),
+        compiler_params=pltpu.CompilerParams(vmem_limit_bytes=60 * 1024 * 1024),
         name="middle",
     )(me, part, x2, mix, dy, gain, router)
 
@@ -472,22 +502,22 @@
 
 
 def finish_kernel(
-    me, qm_ref, qo_ref, km_ref, ko_ref, w0, w1, w2, w3, x_ref, gain_ref, da_ref,
+    me, m_ref, o_ref, w0, w1, w2, w3, x_ref, gain_ref, da_ref,
     early_ref, gkv_ref, rest_ref, out_ref, small_ref,
 ):
     xh = me[1]
 
-    def back(q_ref, kv_ref, side, w):
-        left = lax.broadcasted_iota(jnp.int32, kv_ref.shape[1:], 1) < 64
-        one, two = kv_ref[side].astype(F32), kv_ref[2 + side].astype(F32)
-        keys = jnp.where(left, one, pltpu.roll(two, 64, 1)).astype(BF16)
-        values = jnp.where(left, pltpu.roll(one, 64, 1), two).astype(BF16)
-        return inner(
-            jnp.concatenate([q_ref[side], q_ref[2 + side], keys, values], 1), w[...]
-        )
-
-    near = back(qm_ref, km_ref, xh, w0) + back(qo_ref, ko_ref, xh, w1)
-    far = back(qm_ref, km_ref, 1 - xh, w2) + back(qo_ref, ko_ref, 1 - xh, w3)
+    def back(ref, side, w):
+        one, two = ref[side], ref[2 + side]
+        hq = one.shape[1] // 2
+        left = lax.broadcasted_iota(jnp.int32, (one.shape[0], hq), 1) < 64
+        low, high = one[:, hq:].astype(F32), two[:, hq:].astype(F32)
+        keys = jnp.where(left, low, pltpu.roll(high, 64, 1)).astype(BF16)
+        values = jnp.where(left, pltpu.roll(low, 64, 1), high).astype(BF16)
+        return inner(jnp.concatenate([one[:, :hq], two[:, :hq], keys, values], 1), w[...])
+
+    near = back(m_ref, xh, w0) + back(o_ref, xh, w1)
+    far = back(m_ref, 1 - xh, w2) + back(o_ref, 1 - xh, w3)
     dh1 = near + far
     x = x_ref[...].astype(F32)
     factor = lax.rsqrt(jnp.mean(x * x, -1, keepdims=True) + EPS)
@@ -507,9 +537,9 @@
     small_ref[:, 384:] = jnp.where(lane == mark, column, rest_ref[...].astype(F32)).astype(BF16)
 
 
-def finish(me, qm, qo, km, ko, ws, tokens, gain, da, early, gkv, rest):
+def finish(me, mine, other, ws, tokens, gain, da, early, gkv, rest):
     rows, width = tokens.shape
-    args = (qm, qo, km, ko, *ws, tokens, gain)
+    args = (mine, other, *ws, tokens, gain)
     shapes = [
         jax.ShapeDtypeStruct((rows, width), BF16),
         jax.ShapeDtypeStruct((width, 512), BF16),
@@ -528,6 +558,71 @@
         compiler_params=pltpu.CompilerParams(vmem_limit_bytes=LIMIT),
         name="finish",
     )(me, *args, da, early, gkv, rest)
+
+
+def unpack_kernel(
+    me, part_ref, keep_ref, got_ref, own_ref, near_ref, far_ref, last_ref,
+    q_ref, k_ref, v_ref, o_ref, r_ref, nm_ref, na_ref, gate_ref, up_ref, down_ref, out_ref,
+):
+    local, few = keep_ref.shape[0], own_ref.shape[0]
+    for ref, side in ((keep_ref, me[0]), (got_ref, 1 - me[0])):
+        for e in range(local):
+            gate_ref[side * local + e] = ref[e, : gate_ref.shape[1], : gate_ref.shape[2]].astype(F32)
+            up_ref[side * local + e] = ref[e, : gate_ref.shape[1], gate_ref.shape[2] :].astype(F32)
+            down_ref[side * local + e] = ref[e, gate_ref.shape[1] :, :].astype(F32)
+    for ref, xh, core in (
+        (own_ref, me[1], me[2]),
+        (near_ref, me[1], 1 - me[2]),
+        (far_ref, 1 - me[1], me[2]),
+        (last_ref, 1 - me[1], 1 - me[2]),
+    ):
+        out_ref[pl.ds(pl.multiple_of((xh * 2 + core) * few, few), few), :] = ref[...]
+    groups = part_ref.shape[0] // 2
+    sums = []
+    for side in (0, 1):
+        total = part_ref[side].astype(F32)
+        for j in range(1, groups):
+            total = total + part_ref[2 * j + side].astype(F32)
+        sums.append(total)
+    one, two = sums
+    q_ref[...] = jnp.concatenate([one[:, :128], two[:, :128]], 1)
+    o_ref[...] = jnp.concatenate([one[:, 128:256], two[:, 128:256]], 1)
+    left = lax.broadcasted_iota(jnp.int32, (one.shape[0], 128), 1) < 64
+    low, high = one[:, 256:384], two[:, 256:384]
+    k_ref[...] = jnp.where(left, low, pltpu.roll(high, 64, 1))
+    v_ref[...] = jnp.where(left, pltpu.roll(low, 64, 1), high)
+    rest = one[:, 384:] + two[:, 384:]
+    rest = jnp.concatenate([rest, jnp.zeros((128 - rest.shape[0], 128), F32)], 0).T
+    rows = q_ref.shape[0]
+    count = r_ref.shape[0]
+    r_ref[...] = rest[:count, :rows]
+    nm_ref[...] = rest[count : count + 1, :rows]
+    na_ref[...] = rest[127:, :rows]
+
+
+def unpack(me, part, keep, got, outs, experts_all):
+    rows = part.shape[1]
+    local, width = keep.shape[0], keep.shape[2]
+    args = (part, keep, got, *outs)
+    shapes = [
+        jax.ShapeDtypeStruct(n, F32)
+        for n in (
+            (rows, 256), (rows, 128), (rows, 128), (rows, 256), (experts_all, rows), (1, rows), (1, rows),
+            (2 * local, rows, width // 2), (2 * local, rows, width // 2), (2 * local, rows // 2, width),
+        )
+    ] + [jax.ShapeDtypeStruct((4 * outs[0].shape[0], width), BF16)]
+    return pl.pallas_call(
+        unpack_kernel,
+        grid_spec=pltpu.PrefetchScalarGridSpec(
+            num_scalar_prefetch=1,
+            grid=(1,),
+            in_specs=[whole(a) for a in args],
+            out_specs=[whole(a) for a in shapes],
+        ),
+        out_shape=shapes,
+        compiler_params=pltpu.CompilerParams(vmem_limit_bytes=LIMIT),
+        name="unpack",
+    )(me, *args)
 
 
 def on_device(
@@ -589,27 +684,27 @@
         return w, near, far, lax.ppermute(far, "c", SWAP)
 
     w_outs = ring_weights(w_out)
-    w_ins = ring_weights(jnp.concatenate([w_query, w_key, w_value], 1))
+    w_in = jnp.concatenate([w_query, w_key, w_value], 1)
 
     def ring_parts(w):
         return w, lax.ppermute(w, "c", SWAP), lax.ppermute(w, "xh", SWAP), lax.ppermute(
             w, WA, [(0, 3), (3, 0), (1, 2), (2, 1)]
         )
 
-    def in_order(parts):
-        near = jnp.where(core == 0, jnp.concatenate(parts[:2], 0), jnp.concatenate(parts[1::-1], 0))
-        far = jnp.where(core == 0, jnp.concatenate(parts[2:], 0), jnp.concatenate(parts[:1:-1], 0))
-        return jnp.where(xh == 0, jnp.concatenate([near, far], 0), jnp.concatenate([far, near], 0))
-
     x_pair = swap_x(tokens)
+    routes_pair = swap_x(routes.astype(F32)).astype(jnp.int32)
+    h1 = rms(x_pair.astype(F32), norm_attn)[0].astype(BF16)
+    kv_all, x_pair, routes_pair, h1, cotangent = lax.optimization_barrier(
+        (kv_all, x_pair, routes_pair, h1, cotangent)
+    )
     dy_pair = swap_x(cotangent)
-    routes_pair = swap_x(routes.astype(F32)).astype(jnp.int32)
 
     ranks = jnp.arange(count_ctx, dtype=jnp.int32)
     inverse = jnp.sum(jnp.where(pairing[None, :] == ranks[:, None], ranks[None, :], 0), 1)
     slot = jnp.concatenate([inverse * 2, inverse[::-1] * 2 + 1])
     place = starts // block
     attn_low, attn, lse, ks, kt = attend(place, slot, rq, kv_all)
+    attn_low, dy_pair, w_outs = lax.optimization_barrier((attn_low, dy_pair, w_outs))
 
     o_mine = lax.all_to_all(
         jnp.broadcast_to(attn_low[None], (4,) + attn_low.shape), CHIPS, 0, 0, tiled=False
@@ -632,41 +727,45 @@
     full = lax.all_to_all(payload, CHIPS, 0, 0, tiled=False)
     other = lax.ppermute(full, "c", SWAP)
 
-    moe = add(mkeep, lax.ppermute(mgive, "c", SWAP))
-    moe, full = lax.optimization_barrier((moe, full))
-    moe = lax.all_to_all(moe, CHIPS, 0, 0, tiled=False)
+    full, w_in = lax.optimization_barrier((full, w_in))
+    w_ins = ring_weights(w_in)
 
     dq, grad_kv, da, rest_pair = attend_back(
         place, slot, me, rq, full, other, attn, lse, ks, kt, cos2, sin2, w_out
     )
+    grad_kv, mkeep, mgot = lax.optimization_barrier(
+        (grad_kv, mkeep, lax.ppermute(mgive, "c", SWAP))
+    )
+    moe = add(mkeep, mgot).reshape(2, 2, both // 8, width)
+    at = lambda a, b: lax.dynamic_index_in_dim(
+        lax.dynamic_index_in_dim(moe, a, 0, False), b, 0, False
+    )
     few = both // 8
-    mine = lambda a: lax.dynamic_slice_in_dim(a, (xl * 4 + wa) * few, few, 0)
-    out_rows = (mine(x2) + jnp.sum(moe.astype(F32), 0)).astype(BF16)
-    ones = ring_parts(out_rows)
-    output = in_order(ones)
+    moe_rows = (
+        at(xl, xh).astype(F32)
+        + lax.ppermute(at(1 - xl, xh), "xl", SWAP).astype(F32)
+        + lax.ppermute(at(xl, 1 - xh), "xh", SWAP).astype(F32)
+        + lax.ppermute(at(1 - xl, 1 - xh), CHIPS, [(0, 3), (3, 0), (1, 2), (2, 1)]).astype(F32)
+    )
+    out_rows = (lax.dynamic_slice_in_dim(x2, me[4] * few, few, 0) + moe_rows).astype(BF16)
     gnm_all = rest_pair[:, experts_all : experts_all + width // few].astype(F32)
     gnm_own = jnp.sum(own(gnm_all).reshape(4, few, width // few), 0).reshape(width)
     grad_kv = lax.all_to_all(
         grad_kv.reshape(groups, both, 2 * hk), ZY, 0, 0, tiled=False
     )
-    grad_kv, grads = lax.optimization_barrier((grad_kv, grads))
+    h2_own = own(h2)
+    rest = jnp.concatenate(
+        [outer(h2_own, own(rest_pair)[:, :experts_all]), gnm_own[:, None]], 1
+    ).astype(BF16)
+    rest = jnp.pad(rest, ((0, 0), (0, 128 - rest.shape[1])))
+    early = jnp.concatenate([outer(h1, dq), outer(da, attn_low)], 1).astype(BF16)
+    grad_kv, rest, early, out_rows, w_ins, grads = lax.optimization_barrier(
+        (grad_kv, rest, early, out_rows, w_ins, grads)
+    )
     grads = lax.psum_scatter(grads, "y", scatter_dimension=0, tiled=True)[0]
     dkv = collect(grad_kv, cos2, sin2)
-    h1 = rms(x_pair.astype(F32), norm_attn)[0].astype(BF16)
 
     def to_rows(piece):
-        n = piece.shape[1]
-        parts = piece.reshape(2, rows, n)
-        same = lax.dynamic_index_in_dim(parts, xl, 0, False)
-        swapped = lax.ppermute(lax.dynamic_index_in_dim(parts, 1 - xl, 0, False), "xl", SWAP)
-        both_far = lax.ppermute(jnp.stack([same, swapped]), "xh", SWAP)
-        here = jnp.where(low, jnp.stack([same, swapped]), jnp.stack([swapped, same]))
-        away = jnp.where(low, both_far, both_far[::-1])
-        mine = jnp.where(xh == 0, jnp.stack([here, away], 1), jnp.stack([away, here], 1))
-        mine = mine.reshape(4, rows, n)
-        return mine, lax.ppermute(mine, "c", SWAP)
-
-    def to_rows_now(piece):
         n = piece.shape[1]
         mine = lax.all_to_all(
             jnp.broadcast_to(piece.reshape(2, 1, rows, n), (2, 2, rows, n)).reshape(4, rows, n),
@@ -674,17 +773,10 @@
         )
         return mine, lax.ppermute(mine, "c", SWAP)
 
-    dq_mine, dq_other = to_rows(dq)
-    kv_mine, kv_other = to_rows_now(dkv)
-    h2_own = own(h2)
-    rest = jnp.concatenate(
-        [outer(h2_own, own(rest_pair)[:, :experts_all]), gnm_own[:, None]], 1
-    ).astype(BF16)
-    rest = jnp.pad(rest, ((0, 0), (0, 128 - rest.shape[1])))
-    early = jnp.concatenate([outer(h1, dq), outer(da, attn_low)], 1).astype(BF16)
+    d_mine, d_other = to_rows(jnp.concatenate([dq, dkv], 1))
     gkv = outer(h1, dkv).astype(BF16)
     grad_tokens, small = finish(
-        me, dq_mine, dq_other, kv_mine, kv_other, w_ins, tokens, norm_attn[None], da,
+        me, d_mine, d_other, w_ins, tokens, norm_attn[None], da,
         early, gkv, rest,
     )
 
@@ -697,30 +789,18 @@
         ],
         2,
     ).transpose(1, 0, 2, 3)
-    by_dest, small = lax.optimization_barrier((by_dest, small))
+    by_dest, small, out_rows = lax.optimization_barrier((by_dest, small, out_rows))
+    outs = ring_parts(out_rows)
     keep_w = lax.dynamic_index_in_dim(by_dest, xl, 0, False)
     got_w = lax.ppermute(lax.dynamic_index_in_dim(by_dest, 1 - xl, 0, False), "xl", SWAP)
 
     small = lax.all_to_all(small.reshape(count_ctx, -1, small.shape[1]), CTX, 0, 0, tiled=False)
-    small = jnp.sum(small.reshape(groups, 2, -1, small.shape[2]).astype(F32), 0)
-    def pair_of(a, n):
-        return jnp.concatenate([small[0, :, a : a + n], small[1, :, a : a + n]], 1)
-
-    grad_query = pair_of(0, hq)
-    grad_out = pair_of(hq, hq).T
-    grad_key = pair_of(2 * hq, hk)
-    grad_value = pair_of(2 * hq + hk, hk)
-    rest = small[0, :, 3 * hq :] + small[1, :, 3 * hq :]
-    grad_router = rest[:, :experts_all]
-    grad_norm_moe = rest[:, experts_all]
-    grad_norm_attn = rest[:, 127]
-    pairw = jnp.concatenate(
-        [jnp.where(low, keep_w, got_w), jnp.where(low, got_w, keep_w)], 0
-    ).astype(F32)
-    half = width // 2
-    grad_gate = pairw[:, :nrow, :half]
-    grad_up = pairw[:, :nrow, half:]
-    grad_down = pairw[:, nrow:]
+    (
+        grad_query, grad_key, grad_value, grad_out, grad_router, gnm, gna, grad_gate, grad_up,
+        grad_down, output,
+    ) = unpack(me, small, keep_w, got_w, outs, experts_all)
+    grad_out, grad_router = grad_out.T, grad_router.T
+    grad_norm_moe, grad_norm_attn = gnm.reshape(-1), gna.reshape(-1)
     return (
         output,
         grad_tokens,

time: 327 us -> 275 us (0.84)
  waiting for transfers between devices: 92.6 us -> 56.3 us
  blocking collectives: 12.8 us -> 44.9 us
  local copies, waits for them, and re-layouts: 34.4 us -> 15.6 us
  other arithmetic: 25.6 us -> 15.1 us
  starting transfers between devices: 66.2 us -> 56 us
  Pallas kernels: 75.2 us -> 66.4 us
    all_to_all x0 -> x3, blocking collectives: none -> 32.2 us  [the longest x1 12.2 us: on_device(): full = lax.all_to_all(payload, CHIPS, 0, 0, tiled=False)]
    all_to_all x1, waiting for transfers between devices: 23.7 us -> 0.01 us  [on_device(): lax.all_to_all(jnp.broadcast_to(kv_mine[None], (groups,) + kv_mine.shape)...]
    all_to_all x4 -> x0, waiting for transfers between devices: 16.8 us -> none  [the longest x1 8.29 us: on_device(): full = lax.all_to_all(payload, CHIPS, 0, 0, tiled=False)]
    all_to_all x4 -> x0, starting transfers between devices: 15.4 us -> none  [the longest x1 4.28 us: on_device(): moe = lax.all_to_all(moe, CHIPS, 0, 0, tiled=False)]
    all_to_all x1, waiting for transfers between devices: 27.7 us -> 13.1 us  [on_device(): lax.all_to_all(grad_kv.reshape(groups, both, 2 * hk), ZY, 0, 0, tiled=False)]
    ppermute x1, waiting for transfers between devices: 0.01 us -> 13.9 us  [ring_parts(): lax.ppermute(w, 'xh', SWAP)]
    unnamed x98 -> x57, local copies, waits for them, and re-layouts: 20.3 us -> 6.64 us
    ppermute x1, waiting for transfers between devices: 12.6 us -> 0.01 us  [on_device(): lax.ppermute(lax.dynamic_index_in_dim(by_dest, 1 - xl, 0, False), 'xl', S...]
  transfers between devices with their start and end apart: 31 -> 27, of which waited for: 10 -> 10; matrix products, arithmetic and copies ran while one was open for 12% -> 8% of each run, Pallas kernels for 16% -> 14%
where the time goes in v1:
time: 275 us; the launch traced here: 274 us
  Pallas kernels  66.4 us (24%)
  waiting for transfers between devices  56.3 us (20%)
  starting transfers between devices  56 us (20%)
  blocking collectives  44.9 us (16%)
  local copies, waits for them, and re-layouts  15.6 us (6%)
  other arithmetic  15.1 us (5%)
  between operations  14.5 us (5%)
  matrix products  5.54 us (2%)
    pallas_call x1, Pallas kernels, experts(): pl.pallas_call(experts_kernel, grid_spec=pltpu.PrefetchScalarGridSpec(num...  22.1 us
    ppermute x3, waiting for transfers between devices, swap_x(): other = lax.ppermute(mine, 'xl', SWAP)  16.7 us
    pallas_call x1, Pallas kernels, attend_back(): pl.pallas_call(attend_back_kernel, grid_spec=pltpu.PrefetchScalarGridSpec...  16.6 us
    ppermute x1, waiting for transfers between devices, ring_parts(): lax.ppermute(w, 'xh', SWAP)  13.9 us
    all_to_all x1, waiting for transfers between devices, on_device(): lax.all_to_all(grad_kv.reshape(groups, both, 2 * hk), ZY, 0, 0, tiled=False)  13.1 us
    pallas_call x1, Pallas kernels, attend(): pl.pallas_call(attend_kernel, grid_spec=pltpu.PrefetchScalarGridSpec(num_...  12.8 us
    all_to_all x1, blocking collectives, on_device(): part = lax.all_to_all(part, CHIPS, 0, 0, tiled=False)  12.7 us
    all_to_all x1, blocking collectives, on_device(): full = lax.all_to_all(payload, CHIPS, 0, 0, tiled=False)  12.2 us
  transfers between devices with their start and end apart: 27, of which 10 were waited for; matrix products, arithmetic and copies ran while one was open for 8% of the time, Pallas kernels for 14%

profile of v1, /device:TPU:1, one launch (start us, length us, event | category | flops | bytes accessed | tf_op | source)
XLA Modules:
  0.0 274.3 jit_solution(3101921637985113969)
XLA Ops:
  11.2 3.6 %start.1 = (bf16[256,256]{1,0:T(8,128)(2,1)}, bf16[256,256]{1,0:T(8,128)(2,1)}) custom-call(s32[5]{0:T(128)} %stack.32.me, bf16[256,1024]{1,0:T(8,128)(2,1)} %x_ref.3, f32[1,1024]{1,0:T(1,128)} %bitcast.49, bf16[1024,256]{1,0:T(8,128)(2,1)} %wq_ref.1, bf16[1024,128]{1,0:T(8,128)(2,1)} %wk_ref.1, bf16[1024,128]{1,0:T(8,128)(2,1)} %wv_ref.1, ...), custom_call_target="tpu_custom_call" | custom-call | tf_op jit(solution)/shard_map/start/pallas_call | solution.py:414
  16.9 2.9 %collective-permute-done = bf16[256,256]{1,0:T(8,128)(2,1)S(1)} collective-permute-done((bf16[256,256]{1,0:T(8,128)(2,1)}, bf16[256,256]{1,0:T(8,128)(2,1)S(1)}, u32[]{:S(2)}, u32[]{:S(2)}) %collective-permute-start) | collective-permute-done | bytes 131104 | tf_op jit(solution)/shard_map/ppermute | solution.py:671
  22.6 8.4 %all-to-all-start = ((bf16[16,512,128]{2,1,0:T(8,128)(2,1)}), bf16[16,512,128]{2,1,0:T(8,128)(2,1)}, u32[]{:S(2)}, u32[]{:S(2)}) async-start(bf16[16,512,128]{2,1,0:T(8,128)(2,1)} %broadcast_in_dim.62), calls=%async_computation | async-start | bytes 4194304 | tf_op jit(solution)/shard_map/all_to_all | solution.py:677
  32.3 2.5 collective-permute-start.5
  37.5 16.7 %collective-permute-done.2 = f32[256,8]{0,1:T(8,128)S(1)} collective-permute-done((f32[256,8]{0,1:T(8,128)S(1)}, f32[256,8]{0,1:T(8,128)S(1)}, u32[]{:S(2)}, u32[]{:S(2)}) %collective-permute-start.2) | collective-permute-done | bytes 8224 | tf_op jit(solution)/shard_map/ppermute | solution.py:39
  56.2 2.8 %collective-permute-start.6 = (bf16[256,1024]{1,0:T(8,128)(2,1)}, bf16[256,1024]{1,0:T(8,128)(2,1)}, u32[]{:S(2)}, u32[]{:S(2)}) collective-permute-start(bf16[256,1024]{1,0:T(8,128)(2,1)} %collective-permute-done.5.wo2), channel_id=1, source_target_pairs={{0,1},{1,0},{2,3},{3,2},{4,5},{5,4},{6,7},{7,6},{8,9},{9,8},{10,11... | collective-permute-start | bytes 1572872 | tf_op jit(solution)/shard_map/ppermute | solution.py:684
  61.8 12.8 %attend.1 = (bf16[512,128]{1,0:T(8,128)(2,1)S(1)}, f32[4,64,256]{2,1,0:T(8,128)S(1)}, f32[4,1,256]{2,1,0:T(1,128)S(1)}, bf16[8,1024,128]{2,1,0:T(8,128)(2,1)S(1)}, bf16[8,128,1024]{2,1,0:T(8,128)(2,1)S(1)}) custom-call(s32[4]{0:T(128)S(1)} %and_select_fusion.2.place, s32[64]{0:T(128)S(1)} %pad_add_fusion.slot, ...), custom_call_target="tpu_custom_call" | custom-call | flops 20000000000 | bytes 8000000 | tf_op jit(solution)/shard_map/attend/pallas_call | solution.py:142
  77.4 10.0 %all_to_all.35.o_ref = bf16[4,512,128]{2,1,0:T(8,128)(2,1)S(1)} all-to-all(bf16[4,512,128]{2,1,0:T(8,128)(2,1)S(1)} %broadcast_in_dim.63), channel_id=1, replica_groups=mesh['z'=4,'y'=4,'xl'=2,'xh'=2,'c'=2] {'xl','xh'}, dimensions={0} | all-to-all | bytes 1048576 | tf_op jit(solution)/shard_map/all_to_all | solution.py:709
  87.4 3.9 %collective-permute-start.7 = (bf16[4,512,128]{2,1,0:T(8,128)(2,1)S(1)}, bf16[4,512,128]{2,1,0:T(8,128)(2,1)S(1)}, u32[]{:S(2)}, u32[]{:S(2)}) collective-permute-start(bf16[4,512,128]{2,1,0:T(8,128)(2,1)S(1)} %all_to_all.35.o_ref), channel_id=1, source_target_pairs={{0,1},{1,0},{2,3},{3,2},{4,5},{5,4},{6,7},{7,6},{8,9},{9,8},{10,11... | collective-permute-start | bytes 1572872 | tf_op jit(solution)/shard_map/ppermute | solution.py:712
  93.6 22.1 %experts.1 = (f32[512,1024]{1,0:T(8,128)}, bf16[512,1024]{1,0:T(8,128)(2,1)}, f32[512,128]{1,0:T(8,128)}, bf16[4,64,1152]{2,1,0:T(8,128)(2,1)}, bf16[4,64,1152]{...) custom-call(s32[5]{0:T(128)} %stack.32.me, ...), custom_call_target="tpu_custom_call" | custom-call | flops 20000000000 | bytes 20000000 | tf_op jit(solution)/shard_map/experts/pallas_call | solution.py:366
  120.0 12.7 %all_to_all.36.part_ref = bf16[4,64,1152]{2,1,0:T(8,128)(2,1)} all-to-all(bf16[4,64,1152]{2,1,0:T(8,128)(2,1)S(1)} %add_convert_fusion), channel_id=1, replica_groups=mesh['z'=4,'y'=4,'xl'=2,'xh'=2,'c'=2] {'xl','xh'}, dimensions={0} | all-to-all | bytes 1179648 | tf_op jit(solution)/shard_map/all_to_all | solution.py:724
  132.7 3.4 %middle.1 = bf16[4,64,1152]{2,1,0:T(8,128)(2,1)} custom-call(s32[5]{0:T(128)} %stack.32.me, bf16[4,64,1152]{2,1,0:T(8,128)(2,1)} %all_to_all.36.part_ref, f32[512,1024]{1,0:T(8,128)} %get-tuple-element.87.x2_ref, f32[512,128]{1,0:T(8,128)} %get-tuple-element.88.mix_ref, bf16[512,1024]{1,0:T(8,128)(2,1)} %pad_maximum_fusion.1.dy_ref, f32[1,1024]{1,0:T(1,128)} %bitcast.61, ...), custom_call_target="tpu_custom_call" | custom-call | tf_op jit(solution)/shard_map/middle/pallas_call | solution.py:460
  136.1 12.2 %all_to_all.37.full_ref = bf16[4,64,1152]{2,1,0:T(8,128)(2,1)S(1)} all-to-all(bf16[4,64,1152]{2,1,0:T(8,128)(2,1)} %middle.1), channel_id=1, replica_groups=mesh['z'=4,'y'=4,'xl'=2,'xh'=2,'c'=2] {'xl','xh'}, dimensions={0} | all-to-all | bytes 1179648 | tf_op jit(solution)/shard_map/all_to_all | solution.py:727
  152.8 16.6 %attend_back.1 = (bf16[512,128]{1,0:T(8,128)(2,1)S(1)}, bf16[64,128,128]{2,1,0:T(8,128)(2,1)S(1)}, bf16[512,1024]{1,0:T(8,128)(2,1)S(1)}, bf16[512,128]{1,0:T(8,128)(2,1)S(1)}) custom-call(s32[4]{0:T(128)S(1)} %and_select_fusion.2.place, s32[64]{0:T(128)S(1)} %pad_add_fusion.slot, s32[5]{0:T(128)S(1)} %copy-done.9, ...), custom_call_target="tpu_custom_call" | custom-call | flops 30000001024 | bytes 8000000 | tf_op jit(solution)/shard_map/attend_back/pallas_call | solution.py:250
  172.6 6.3 %all-to-all-start.4 = ((bf16[16,512,128]{2,1,0:T(8,128)(2,1)}), bf16[16,512,128]{2,1,0:T(8,128)(2,1)S(1)}, u32[]{:S(2)}, u32[]{:S(2)}) async-start(bf16[16,512,128]{2,1,0:T(8,128)(2,1)} %bitcast.48), calls=%async_computation.4 | async-start | bytes 4194304 | tf_op jit(solution)/shard_map/all_to_all | solution.py:753
  187.6 2.4 convolution_convert_fusion.1
  195.8 13.1 %all-to-all-done.4.part_ref = bf16[16,512,128]{2,1,0:T(8,128)(2,1)S(1)} async-done(((bf16[16,512,128]{2,1,0:T(8,128)(2,1)}), bf16[16,512,128]{2,1,0:T(8,128)(2,1)S(1)}, u32[]{:S(2)}, u32[]{:S(2)}) %all-to-all-start.4) | async-done | bytes 2097184 | tf_op jit(solution)/shard_map/all_to_all | solution.py:753
  210.9 10.0 %all_to_all.38.m_ref = bf16[4,256,256]{2,1,0:T(8,128)(2,1)S(1)} all-to-all(bf16[4,256,256]{2,1,0:T(8,128)(2,1)S(1)} %bitcast.53), channel_id=1, replica_groups=mesh['z'=4,'y'=4,'xl'=2,'xh'=2,'c'=2] {'xl','xh'}, dimensions={0} | all-to-all | bytes 1048576 | tf_op jit(solution)/shard_map/all_to_all | solution.py:770
  220.9 3.3 %collective-permute-start.17 = (bf16[4,256,256]{2,1,0:T(8,128)(2,1)S(1)}, bf16[4,256,256]{2,1,0:T(8,128)(2,1)S(1)}, u32[]{:S(2)}, u32[]{:S(2)}) collective-permute-start(bf16[4,256,256]{2,1,0:T(8,128)(2,1)S(1)} %all_to_all.38.m_ref), channel_id=1, source_target_pairs={{0,1},{1,0},{2,3},{3,2},{4,5},{5,4},{6,7},{7,6},{8,9},{9,8},{10,11... | collective-permute-start | bytes 1572872 | tf_op jit(solution)/shard_map/ppermute | solution.py:774
  225.7 5.7 %finish.1 = (bf16[256,1024]{1,0:T(8,128)(2,1)}, bf16[1024,512]{1,0:T(8,128)(2,1)}) custom-call(s32[5]{0:T(128)S(1)} %copy-done.9, bf16[4,256,256]{2,1,0:T(8,128)(2,1)S(1)} %all_to_all.38.m_ref, bf16[4,256,256]{2,1,0:T(8,128)(2,1)S(1)} %collective-permute-done.17.o_ref, bf16[1024,512]{1,0:T(8,128)(2,1)} %pad_maximum_fusion.2.w0, ...), custom_call_target="tpu_custom_call" | custom-call | tf_op jit(solution)/shard_map/finish/pallas_call | solution.py:547
  234.4 6.9 %all-to-all-start.6 = ((bf16[32,32,512]{2,1,0:T(8,128)(2,1)}), bf16[32,32,512]{2,1,0:T(8,128)(2,1)S(1)}, u32[]{:S(2)}, u32[]{:S(2)}) async-start(bf16[32,32,512]{2,1,0:T(8,128)(2,1)} %bitcast.24), calls=%async_computation.8 | async-start | bytes 2097152 | tf_op jit(solution)/shard_map/all_to_all | solution.py:797
  244.5 2.4 collective-permute-start.20
  247.7 13.9 %collective-permute-done.20.far_ref = bf16[64,1024]{1,0:T(8,128)(2,1)S(1)} collective-permute-done((bf16[64,1024]{1,0:T(8,128)(2,1)S(1)}, bf16[64,1024]{1,0:T(8,128)(2,1)S(1)}, u32[]{:S(2)}, u32[]{:S(2)}) %collective-permute-start.20) | collective-permute-done | bytes 131104 | tf_op jit(solution)/shard_map/ppermute | solution.py:690
  261.5 4.2 %collective-permute-done.21.last_ref = bf16[64,1024]{1,0:T(8,128)(2,1)S(1)} collective-permute-done((bf16[64,1024]{1,0:T(8,128)(2,1)S(1)}, bf16[64,1024]{1,0:T(8,128)(2,1)S(1)}, u32[]{:S(2)}, u32[]{:S(2)}) %collective-permute-start.21) | collective-permute-done | bytes 131104 | tf_op jit(solution)/shard_map/ppermute | solution.py:690
  (156 shorter events, 61.0 us)
Async XLA Ops:
  14.9 5.0 %collective-permute-start = (bf16[256,256]{1,0:T(8,128)(2,1)}, bf16[256,256]{1,0:T(8,128)(2,1)S(1)}, u32[]{:S(2)}, u32[]{:S(2)}) collective-permute-start(bf16[256,256]{1,0:T(8,128)(2,1)} %get-tuple-element.73), channel_id=1, source_target_pairs={{0,4},{4,0},{1,5},{5,1},{2,6},{6,2},{3,7},{7,3},{8,12},{12,8},{9,1... | collective-permute-start | bytes 393224 | tf_op jit(solution)/shard_map/ppermute | solution.py:671
  22.6 39.3 %all-to-all-start = ((bf16[16,512,128]{2,1,0:T(8,128)(2,1)}), bf16[16,512,128]{2,1,0:T(8,128)(2,1)}, u32[]{:S(2)}, u32[]{:S(2)}) async-start(bf16[16,512,128]{2,1,0:T(8,128)(2,1)} %broadcast_in_dim.62), calls=%async_computation | async-start | bytes 4194304 | tf_op jit(solution)/shard_map/all_to_all | solution.py:677
  31.0 178.0 %reduce-scatter.3.cloned.1.call-start = ((), (), s32[]{:S(2)}) async-start(), calls=%async_computation.9 | async-start | bytes 7864320 | tf_op jit(solution)/shard_map/reduce_scatter | solution.py:725
  31.0 28.0 %collective-permute-start.1 = (bf16[256,1024]{1,0:T(8,128)(2,1)S(1)}, bf16[256,1024]{1,0:T(8,128)(2,1)S(1)}, u32[]{:S(2)}, u32[]{:S(2)}) collective-permute-start(bf16[256,1024]{1,0:T(8,128)(2,1)S(1)} %copy-done), channel_id=1, source_target_pairs={{0,4},{4,0},{1,5},{5,1},{2,6},{6,2},{3,7},{7,3},{8,12},{12,8},{9,1... | collective-permute-start | bytes 1572872 | tf_op jit(solution)/shard_map/ppermute | solution.py:39
  32.3 23.9 %collective-permute-start.5 = (bf16[256,1024]{1,0:T(8,128)(2,1)S(1)}, bf16[256,1024]{1,0:T(8,128)(2,1)}, u32[]{:S(2)}, u32[]{:S(2)}) collective-permute-start(bf16[256,1024]{1,0:T(8,128)(2,1)S(1)} %copy-done.10), channel_id=1, source_target_pairs={{0,2},{2,0},{1,3},{3,1},{4,6},{6,4},{5,7},{7,5},{8,10},{10,8},{9,1... | collective-permute-start | bytes 1572872 | tf_op jit(solution)/shard_map/ppermute | solution.py:683
  34.8 42.5 %collective-permute-start.4 = (bf16[256,1024]{1,0:T(8,128)(2,1)S(1)}, bf16[256,1024]{1,0:T(8,128)(2,1)}, u32[]{:S(2)}, u32[]{:S(2)}) collective-permute-start(bf16[256,1024]{1,0:T(8,128)(2,1)S(1)} %copy-done.10), channel_id=1, source_target_pairs={{0,1},{1,0},{2,3},{3,2},{4,5},{5,4},{6,7},{7,6},{8,9},{9,8},{10,11... | collective-permute-start | bytes 1572872 | tf_op jit(solution)/shard_map/ppermute | solution.py:682
  37.2 17.0 %collective-permute-start.2 = (f32[256,8]{0,1:T(8,128)S(1)}, f32[256,8]{0,1:T(8,128)S(1)}, u32[]{:S(2)}, u32[]{:S(2)}) collective-permute-start(f32[256,8]{0,1:T(8,128)S(1)} %convert_element_type.80), channel_id=1, source_target_pairs={{0,4},{4,0},{1,5},{5,1},{2,6},{6,2},{3,7},{7,3},{8,12},{12,8},{9,1... | collective-permute-start | bytes 24584 | tf_op jit(solution)/shard_map/ppermute | solution.py:39
  56.2 21.0 %collective-permute-start.6 = (bf16[256,1024]{1,0:T(8,128)(2,1)}, bf16[256,1024]{1,0:T(8,128)(2,1)}, u32[]{:S(2)}, u32[]{:S(2)}) collective-permute-start(bf16[256,1024]{1,0:T(8,128)(2,1)} %collective-permute-done.5.wo2), channel_id=1, source_target_pairs={{0,1},{1,0},{2,3},{3,2},{4,5},{5,4},{6,7},{7,6},{8,9},{9,8},{10,11... | collective-permute-start | bytes 1572872 | tf_op jit(solution)/shard_map/ppermute | solution.py:684
  61.8 12.9 %collective-permute-start.3 = (bf16[256,1024]{1,0:T(8,128)(2,1)}, bf16[256,1024]{1,0:T(8,128)(2,1)S(1)}, u32[]{:S(2)}, u32[]{:S(2)}) collective-permute-start(bf16[256,1024]{1,0:T(8,128)(2,1)} %param.15), channel_id=1, source_target_pairs={{0,4},{4,0},{1,5},{5,1},{2,6},{6,2},{3,7},{7,3},{8,12},{12,8},{9,1... | collective-permute-start | bytes 1572872 | tf_op jit(solution)/shard_map/ppermute | solution.py:39
  87.4 5.4 %collective-permute-start.7 = (bf16[4,512,128]{2,1,0:T(8,128)(2,1)S(1)}, bf16[4,512,128]{2,1,0:T(8,128)(2,1)S(1)}, u32[]{:S(2)}, u32[]{:S(2)}) collective-permute-start(bf16[4,512,128]{2,1,0:T(8,128)(2,1)S(1)} %all_to_all.35.o_ref), channel_id=1, source_target_pairs={{0,1},{1,0},{2,3},{3,2},{4,5},{5,4},{6,7},{7,6},{8,9},{9,8},{10,11... | collective-permute-start | bytes 1572872 | tf_op jit(solution)/shard_map/ppermute | solution.py:712
  151.7 20.0 %collective-permute-start.10 = (bf16[4,64,1024]{2,1,0:T(8,128)(2,1)S(1)}, bf16[4,64,1024]{2,1,0:T(8,128)(2,1)S(1)}, u32[]{:S(2)}, u32[]{:S(2)}) collective-permute-start(bf16[4,64,1024]{2,1,0:T(8,128)(2,1)S(1)} %copy-done.26), channel_id=1, source_target_pairs={{0,1},{1,0},{2,3},{3,2},{4,5},{5,4},{6,7},{7,6},{8,9},{9,8},{10,11... | collective-permute-start | bytes 1572872 | tf_op jit(solution)/shard_map/ppermute | solution.py:737
  151.7 34.6 %collective-permute-start.15 = (bf16[1024,512]{1,0:T(8,128)(2,1)}, bf16[1024,512]{1,0:T(8,128)(2,1)}, u32[]{:S(2)}, u32[]{:S(2)}) collective-permute-start(bf16[1024,512]{1,0:T(8,128)(2,1)} %pad_maximum_fusion.2.w0), channel_id=1, source_target_pairs={{0,2},{2,0},{1,3},{3,1},{4,6},{6,4},{5,7},{7,5},{8,10},{10,8},{9,1... | collective-permute-start | bytes 3145736 | tf_op jit(solution)/shard_map/ppermute | solution.py:683
  172.6 36.4 %all-to-all-start.4 = ((bf16[16,512,128]{2,1,0:T(8,128)(2,1)}), bf16[16,512,128]{2,1,0:T(8,128)(2,1)S(1)}, u32[]{:S(2)}, u32[]{:S(2)}) async-start(bf16[16,512,128]{2,1,0:T(8,128)(2,1)} %bitcast.48), calls=%async_computation.4 | async-start | bytes 4194304 | tf_op jit(solution)/shard_map/all_to_all | solution.py:753
  178.8 53.6 %reduce-scatter.5.cloned.1.call-start = ((), (), s32[]{:S(2)}) async-start(), calls=%async_computation.10 | async-start | bytes 1966080 | tf_op jit(solution)/shard_map/reduce_scatter | solution.py:765
  178.9 16.9 %collective-permute-start.14 = (bf16[1024,512]{1,0:T(8,128)(2,1)}, bf16[1024,512]{1,0:T(8,128)(2,1)}, u32[]{:S(2)}, u32[]{:S(2)}) collective-permute-start(bf16[1024,512]{1,0:T(8,128)(2,1)} %pad_maximum_fusion.2.w0), channel_id=1, source_target_pairs={{0,1},{1,0},{2,3},{3,2},{4,5},{5,4},{6,7},{7,6},{8,9},{9,8},{10,11... | collective-permute-start | bytes 3145736 | tf_op jit(solution)/shard_map/ppermute | solution.py:682
  182.3 12.2 %collective-permute-start.11 = (bf16[64,1024]{1,0:T(8,128)(2,1)}, bf16[64,1024]{1,0:T(8,128)(2,1)}, u32[]{:S(2)}, u32[]{:S(2)}) collective-permute-start(bf16[64,1024]{1,0:T(8,128)(2,1)} %get-tuple-element.136), channel_id=1, source_target_pairs={{0,4},{4,0},{1,5},{5,1},{2,6},{6,2},{3,7},{7,3},{8,12},{12,8},{9,1... | collective-permute-start | bytes 393224 | tf_op jit(solution)/shard_map/ppermute | solution.py:746
  182.6 11.9 %collective-permute-start.12 = (bf16[64,1024]{1,0:T(8,128)(2,1)}, bf16[64,1024]{1,0:T(8,128)(2,1)}, u32[]{:S(2)}, u32[]{:S(2)}) collective-permute-start(bf16[64,1024]{1,0:T(8,128)(2,1)} %get-tuple-element.138), channel_id=1, source_target_pairs={{0,2},{2,0},{1,3},{3,1},{4,6},{6,4},{5,7},{7,5},{8,10},{10,8},{9,1... | collective-permute-start | bytes 393224 | tf_op jit(solution)/shard_map/ppermute | solution.py:747
  185.0 9.5 %collective-permute-start.13 = (bf16[64,1024]{1,0:T(8,128)(2,1)}, bf16[64,1024]{1,0:T(8,128)(2,1)}, u32[]{:S(2)}, u32[]{:S(2)}) collective-permute-start(bf16[64,1024]{1,0:T(8,128)(2,1)} %get-tuple-element.137), channel_id=1, source_target_pairs={{0,6},{6,0},{2,4},{4,2},{1,7},{7,1},{3,5},{5,3},{8,14},{14,8},{10,... | collective-permute-start | bytes 393224 | tf_op jit(solution)/shard_map/ppermute | solution.py:748
  186.3 9.5 %collective-permute-start.16 = (bf16[1024,512]{1,0:T(8,128)(2,1)}, bf16[1024,512]{1,0:T(8,128)(2,1)}, u32[]{:S(2)}, u32[]{:S(2)}) collective-permute-start(bf16[1024,512]{1,0:T(8,128)(2,1)} %collective-permute-done.15.w2), channel_id=1, source_target_pairs={{0,1},{1,0},{2,3},{3,2},{4,5},{5,4},{6,7},{7,6},{8,9},{9,8},{10,11... | collective-permute-start | bytes 3145736 | tf_op jit(solution)/shard_map/ppermute | solution.py:684
  234.4 31.3 %all-to-all-start.6 = ((bf16[32,32,512]{2,1,0:T(8,128)(2,1)}), bf16[32,32,512]{2,1,0:T(8,128)(2,1)S(1)}, u32[]{:S(2)}, u32[]{:S(2)}) async-start(bf16[32,32,512]{2,1,0:T(8,128)(2,1)} %bitcast.24), calls=%async_computation.8 | async-start | bytes 2097152 | tf_op jit(solution)/shard_map/all_to_all | solution.py:797
  241.4 24.4 %collective-permute-start.18 = (bf16[2,48,1024]{2,1,0:T(8,128)(2,1)S(1)}, bf16[2,48,1024]{2,1,0:T(8,128)(2,1)S(1)}, u32[]{:S(2)}, u32[]{:S(2)}) collective-permute-start(bf16[2,48,1024]{2,1,0:T(8,128)(2,1)S(1)} %get-tuple-element.139), channel_id=1, source_target_pairs={{0,4},{4,0},{1,5},{5,1},{2,6},{6,2},{3,7},{7,3},{8,12},{12,8},{9,1... | collective-permute-start | bytes 589832 | tf_op jit(solution)/shard_map/ppermute | solution.py:795
  242.7 5.0 %collective-permute-start.19 = (bf16[64,1024]{1,0:T(8,128)(2,1)S(1)}, bf16[64,1024]{1,0:T(8,128)(2,1)S(1)}, u32[]{:S(2)}, u32[]{:S(2)}) collective-permute-start(bf16[64,1024]{1,0:T(8,128)(2,1)S(1)} %fusion.8.own_ref), channel_id=1, source_target_pairs={{0,1},{1,0},{2,3},{3,2},{4,5},{5,4},{6,7},{7,6},{8,9},{9,8},{10,11... | collective-permute-start | bytes 393224 | tf_op jit(solution)/shard_map/ppermute | solution.py:690
  244.5 17.0 %collective-permute-start.20 = (bf16[64,1024]{1,0:T(8,128)(2,1)S(1)}, bf16[64,1024]{1,0:T(8,128)(2,1)S(1)}, u32[]{:S(2)}, u32[]{:S(2)}) collective-permute-start(bf16[64,1024]{1,0:T(8,128)(2,1)S(1)} %fusion.8.own_ref), channel_id=1, source_target_pairs={{0,2},{2,0},{1,3},{3,1},{4,6},{6,4},{5,7},{7,5},{8,10},{10,8},{9,1... | collective-permute-start | bytes 393224 | tf_op jit(solution)/shard_map/ppermute | solution.py:690
  247.0 18.8 %collective-permute-start.21 = (bf16[64,1024]{1,0:T(8,128)(2,1)S(1)}, bf16[64,1024]{1,0:T(8,128)(2,1)S(1)}, u32[]{:S(2)}, u32[]{:S(2)}) collective-permute-start(bf16[64,1024]{1,0:T(8,128)(2,1)S(1)} %fusion.8.own_ref), channel_id=1, source_target_pairs={{0,3},{3,0},{1,2},{2,1},{4,7},{7,4},{5,6},{6,5},{8,11},{11,8},{9,1... | collective-permute-start | bytes 393224 | tf_op jit(solution)/shard_map/ppermute | solution.py:690
  (31 other events, 401.4 us)
Sparse Core Ops, SparseCore 0:
  115.8 63.1 reduce-scatter.2
  209.1 23.3 reduce-scatter.4

commit v2 on v1

--- a/solution.py
+++ b/solution.py
@@ -36,13 +36,17 @@
 
 
 def swap_x(mine):
-    other = lax.ppermute(mine, "xl", SWAP)
+    return in_pair(mine, lax.ppermute(mine, "xl", SWAP))
+
+
+def in_pair(mine, other):
     low = lax.axis_index("xl") == 0
     return jnp.concatenate([jnp.where(low, mine, other), jnp.where(low, other, mine)], 0)
 
 
 TILE = 1024
-LIMIT = 48 * 1024 * 1024
+LIMIT = 40 * 1024 * 1024
+EXPERT_LIMIT = 56 * 1024 * 1024
 
 
 def full_turn(flat, cosine, sine):
@@ -281,7 +285,7 @@
     me, o_ref, p_ref, x_ref, dy_ref, routes_ref, wo0, wo1, wo2, wo3, gain_ref, wr_ref,
     wg_ref, wu_ref, wd_ref,
     x2_ref, h2_ref, mix_ref, keep_ref, give_ref, mkeep_ref, mgive_ref, grad_ref,
-    dh2_acc, moe_acc, dmix_acc,
+    dh2_acc, moe_acc, dmix_acc, mix_s,
 ):
     step = pl.program_id(0)
     xh, core, first = me[1], me[2], me[3]
@@ -296,7 +300,13 @@
         near = dot(heads(o_ref, xh), wo0[...]) + dot(heads(p_ref, xh), wo1[...])
         far = dot(heads(o_ref, 1 - xh), wo2[...]) + dot(heads(p_ref, 1 - xh), wo3[...])
         x2 = x_ref[...].astype(F32) + (near + far)
-        x2_ref[...] = x2
+        few = rows // 8
+        for j in range(8):
+
+            @pl.when(me[4] == j)
+            def _(j=j):
+                x2_ref[...] = x2[j * few : (j + 1) * few]
+
         h2 = rms(x2, gain_ref[...])[0].astype(BF16)
         h2_ref[...] = h2
         logits = dot(h2, wr_ref[...])
@@ -306,13 +316,14 @@
             used = jnp.logical_or(used, lane == routes[:, k : k + 1])
         top = jnp.max(jnp.where(used, logits, -jnp.inf), 1, keepdims=True)
         expd = jnp.where(used, jnp.exp(logits - top), 0.0)
-        mix_ref[...] = expd / jnp.sum(expd, 1, keepdims=True)
+        mix_s[...] = expd / jnp.sum(expd, 1, keepdims=True)
+        mix_ref[...] = mix_s[pl.ds(pl.multiple_of(me[4] * few, few), few), :]
         dh2_acc[...] = jnp.zeros_like(dh2_acc)
         moe_acc[...] = jnp.zeros_like(moe_acc)
         dmix_acc[...] = jnp.zeros_like(dmix_acc)
 
     here = lane == first + step
-    gate = jnp.sum(jnp.where(here, mix_ref[...], 0.0), 1, keepdims=True)
+    gate = jnp.sum(jnp.where(here, mix_s[...], 0.0), 1, keepdims=True)
     h2 = h2_ref[...]
     dy = dy_ref[...].astype(F32)
     ga = dot(h2, wg_ref[0])
@@ -352,17 +363,17 @@
     local = wg.shape[0] // 2
     ff = wg.shape[2]
     args = (o_mine, o_other, x_pair, dy_pair, routes, *wo, gain, router)
-    across = width // groups
     shapes = [
-        jax.ShapeDtypeStruct((rows, width), F32),
+        jax.ShapeDtypeStruct((few, width), F32),
         jax.ShapeDtypeStruct((rows, width), BF16),
-        jax.ShapeDtypeStruct((rows, 128), F32),
+        jax.ShapeDtypeStruct((few, 128), F32),
         jax.ShapeDtypeStruct((4, few, width + 128), BF16),
         jax.ShapeDtypeStruct((4, few, width + 128), BF16),
         jax.ShapeDtypeStruct((4, few, width), BF16),
         jax.ShapeDtypeStruct((4, few, width), BF16),
     ]
     pick = lambda i, me: (me[0] * local + i, 0, 0)
+    across = width // groups
     return pl.pallas_call(
         experts_kernel,
         grid_spec=pltpu.PrefetchScalarGridSpec(
@@ -380,13 +391,14 @@
                 pltpu.VMEM((rows, width), F32),
                 pltpu.VMEM((rows, width), F32),
                 pltpu.VMEM((rows, 128), F32),
+                pltpu.VMEM((rows, 128), F32),
             ],
         ),
         out_shape=shapes
         + [jax.ShapeDtypeStruct((groups, local, across * 3 // 2, width), BF16)],
-        compiler_params=pltpu.CompilerParams(vmem_limit_bytes=56 * 1024 * 1024),
+        compiler_params=pltpu.CompilerParams(vmem_limit_bytes=EXPERT_LIMIT),
         cost_estimate=pl.CostEstimate(
-            flops=20_000_000_000, bytes_accessed=20_000_000, transcendentals=1_000_000
+            flops=15_000_000_000, bytes_accessed=20_000_000, transcendentals=1_000_000
         ),
         name="experts",
     )(me, *args, wg, wu, wd)
@@ -464,8 +476,8 @@
             grid=(1,),
             in_specs=[
                 whole(part),
-                pl.BlockSpec((few, width), mine),
-                pl.BlockSpec((few, 128), mine),
+                whole(x2),
+                whole(mix),
                 pl.BlockSpec((few, width), mine),
                 whole(gain),
                 whole(router),
@@ -473,7 +485,7 @@
             out_specs=whole(shape),
         ),
         out_shape=shape,
-        compiler_params=pltpu.CompilerParams(vmem_limit_bytes=60 * 1024 * 1024),
+        compiler_params=pltpu.CompilerParams(vmem_limit_bytes=LIMIT),
         name="middle",
     )(me, part, x2, mix, dy, gain, router)
 
@@ -684,7 +696,6 @@
         return w, near, far, lax.ppermute(far, "c", SWAP)
 
     w_outs = ring_weights(w_out)
-    w_in = jnp.concatenate([w_query, w_key, w_value], 1)
 
     def ring_parts(w):
         return w, lax.ppermute(w, "c", SWAP), lax.ppermute(w, "xh", SWAP), lax.ppermute(
@@ -697,22 +708,25 @@
     kv_all, x_pair, routes_pair, h1, cotangent = lax.optimization_barrier(
         (kv_all, x_pair, routes_pair, h1, cotangent)
     )
-    dy_pair = swap_x(cotangent)
+    dy_other = lax.ppermute(cotangent, "xl", SWAP)
 
     ranks = jnp.arange(count_ctx, dtype=jnp.int32)
     inverse = jnp.sum(jnp.where(pairing[None, :] == ranks[:, None], ranks[None, :], 0), 1)
     slot = jnp.concatenate([inverse * 2, inverse[::-1] * 2 + 1])
     place = starts // block
     attn_low, attn, lse, ks, kt = attend(place, slot, rq, kv_all)
-    attn_low, dy_pair, w_outs = lax.optimization_barrier((attn_low, dy_pair, w_outs))
+    attn_low, dy_other, w_outs = lax.optimization_barrier((attn_low, dy_other, w_outs))
+    dy_pair = in_pair(cotangent, dy_other)
 
     o_mine = lax.all_to_all(
         jnp.broadcast_to(attn_low[None], (4,) + attn_low.shape), CHIPS, 0, 0, tiled=False
     )
+    w_in = jnp.concatenate([w_query, w_key, w_value], 1)
+    o_mine, w_in, dy_pair = lax.optimization_barrier((o_mine, w_in, dy_pair))
     o_other = lax.ppermute(o_mine, "c", SWAP)
     experts_all = w_router.shape[1]
     router = jnp.pad(w_router, ((0, 0), (0, 128 - experts_all)))
-    x2, h2, mix_all, keep, give, mkeep, mgive, grads = experts(
+    x2_rows, h2, mix_rows, keep, give, mkeep, mgive, grads = experts(
         me, o_mine, o_other, x_pair, dy_pair, routes_pair, w_outs, norm_moe[None], router,
         w_gate, w_up, w_down, groups,
     )
@@ -723,18 +737,17 @@
     part = add(keep, lax.ppermute(give, "c", SWAP))
     part = lax.all_to_all(part, CHIPS, 0, 0, tiled=False)
     grads = lax.psum_scatter(grads, "z", scatter_dimension=0, tiled=True)
-    payload = middle(me, part, x2, mix_all, dy_pair, norm_moe[None], router)
+    payload = middle(me, part, x2_rows, mix_rows, dy_pair, norm_moe[None], router)
     full = lax.all_to_all(payload, CHIPS, 0, 0, tiled=False)
     other = lax.ppermute(full, "c", SWAP)
 
-    full, w_in = lax.optimization_barrier((full, w_in))
+    w_in, _ = lax.optimization_barrier((w_in, full))
     w_ins = ring_weights(w_in)
-
     dq, grad_kv, da, rest_pair = attend_back(
         place, slot, me, rq, full, other, attn, lse, ks, kt, cos2, sin2, w_out
     )
-    grad_kv, mkeep, mgot = lax.optimization_barrier(
-        (grad_kv, mkeep, lax.ppermute(mgive, "c", SWAP))
+    mkeep, mgot, _ = lax.optimization_barrier(
+        (mkeep, lax.ppermute(mgive, "c", SWAP), grad_kv)
     )
     moe = add(mkeep, mgot).reshape(2, 2, both // 8, width)
     at = lambda a, b: lax.dynamic_index_in_dim(
@@ -747,7 +760,7 @@
         + lax.ppermute(at(xl, 1 - xh), "xh", SWAP).astype(F32)
         + lax.ppermute(at(1 - xl, 1 - xh), CHIPS, [(0, 3), (3, 0), (1, 2), (2, 1)]).astype(F32)
     )
-    out_rows = (lax.dynamic_slice_in_dim(x2, me[4] * few, few, 0) + moe_rows).astype(BF16)
+    out_rows = (x2_rows + moe_rows).astype(BF16)
     gnm_all = rest_pair[:, experts_all : experts_all + width // few].astype(F32)
     gnm_own = jnp.sum(own(gnm_all).reshape(4, few, width // few), 0).reshape(width)
     grad_kv = lax.all_to_all(
@@ -759,8 +772,9 @@
     ).astype(BF16)
     rest = jnp.pad(rest, ((0, 0), (0, 128 - rest.shape[1])))
     early = jnp.concatenate([outer(h1, dq), outer(da, attn_low)], 1).astype(BF16)
-    grad_kv, rest, early, out_rows, w_ins, grads = lax.optimization_barrier(
-        (grad_kv, rest, early, out_rows, w_ins, grads)
+    outs = ring_parts(out_rows)
+    grad_kv, rest, early, outs, w_ins, grads = lax.optimization_barrier(
+        (grad_kv, rest, early, outs, w_ins, grads)
     )
     grads = lax.psum_scatter(grads, "y", scatter_dimension=0, tiled=True)[0]
     dkv = collect(grad_kv, cos2, sin2)
@@ -789,8 +803,7 @@
         ],
         2,
     ).transpose(1, 0, 2, 3)
-    by_dest, small, out_rows = lax.optimization_barrier((by_dest, small, out_rows))
-    outs = ring_parts(out_rows)
+    by_dest, _ = lax.optimization_barrier((by_dest, small))
     keep_w = lax.dynamic_index_in_dim(by_dest, xl, 0, False)
     got_w = lax.ppermute(lax.dynamic_index_in_dim(by_dest, 1 - xl, 0, False), "xl", SWAP)
 

time: 275 us -> 258 us (0.938)
  blocking collectives: 44.9 us -> 32.8 us
  local copies, waits for them, and re-layouts: 15.6 us -> 22.3 us
  Pallas kernels: 66.4 us -> 61 us
  starting transfers between devices: 56 us -> 50.7 us
  waiting for transfers between devices: 56.3 us -> 51.4 us
    all_to_all x1, waiting for transfers between devices: 0.01 us -> 13.7 us  [on_device(): lax.all_to_all(small.reshape(count_ctx, -1, small.shape[1]), CTX, 0, 0, t...]
    ppermute x1, waiting for transfers between devices: 13.9 us -> 1.37 us  [ring_parts(): lax.ppermute(w, 'xh', SWAP)]
    all_to_all x1, waiting for transfers between devices: 0.01 us -> 10.4 us  [on_device(): lax.all_to_all(jnp.broadcast_to(kv_mine[None], (groups,) + kv_mine.shape)...]
    all_to_all x1 -> x0, blocking collectives: 10 us -> none  [on_device(): lax.all_to_all(jnp.broadcast_to(attn_low[None], (4,) + attn_low.shape), C...]
    all_to_all x1, waiting for transfers between devices: 13.1 us -> 4.34 us  [on_device(): lax.all_to_all(grad_kv.reshape(groups, both, 2 * hk), ZY, 0, 0, tiled=False)]
    ppermute x3, waiting for transfers between devices: 16.7 us -> 8.03 us  [the longest x2 8.03 us: swap_x(): return in_pair(mine, lax.ppermute(mine, 'xl', SWAP))]
    unnamed x57 -> x81, local copies, waits for them, and re-layouts: 6.64 us -> 11.3 us
    all_to_all x0 -> x1, waiting for transfers between devices: none -> 4.18 us  [on_device(): lax.all_to_all(jnp.broadcast_to(attn_low[None], (4,) + attn_low.shape), C...]
  transfers between devices with their start and end apart: 27 -> 28, of which waited for: 10 -> 13; matrix products, arithmetic and copies ran while one was open for 8% -> 11% of each run, Pallas kernels for 14% -> 13%
where the time goes in v2:
time: 258 us; the launch traced here: 256 us
  Pallas kernels  61 us (24%)
  waiting for transfers between devices  51.4 us (20%)
  starting transfers between devices  50.7 us (20%)
  blocking collectives  32.8 us (13%)
  local copies, waits for them, and re-layouts  22.3 us (9%)
  other arithmetic  17.6 us (7%)
  between operations  14.6 us (6%)
  matrix products  5.35 us (2%)
    pallas_call x1, Pallas kernels, experts(): pl.pallas_call(experts_kernel, grid_spec=pltpu.PrefetchScalarGridSpec(num...  21.6 us
    pallas_call x1, Pallas kernels, attend_back(): pl.pallas_call(attend_back_kernel, grid_spec=pltpu.PrefetchScalarGridSpec...  15 us
    all_to_all x1, waiting for transfers between devices, on_device(): lax.all_to_all(small.reshape(count_ctx, -1, small.shape[1]), CTX, 0, 0, t...  13.7 us
    all_to_all x1, blocking collectives, on_device(): part = lax.all_to_all(part, CHIPS, 0, 0, tiled=False)  11.8 us
    unnamed x81, local copies, waits for them, and re-layouts  11.3 us
    pallas_call x1, Pallas kernels, attend(): pl.pallas_call(attend_kernel, grid_spec=pltpu.PrefetchScalarGridSpec(num_...  11.2 us
    all_to_all x1, blocking collectives, on_device(): full = lax.all_to_all(payload, CHIPS, 0, 0, tiled=False)  10.7 us
    all_to_all x1, waiting for transfers between devices, on_device(): lax.all_to_all(jnp.broadcast_to(kv_mine[None], (groups,) + kv_mine.shape)...  10.4 us
  transfers between devices with their start and end apart: 28, of which 13 were waited for; matrix products, arithmetic and copies ran while one was open for 11% of the time, Pallas kernels for 13%

profile of v2, /device:TPU:1, one launch (start us, length us, event | category | flops | bytes accessed | tf_op | source)
XLA Modules:
  0.0 255.7 jit_solution(6704722908623761227)
XLA Ops:
  11.3 3.6 %start.1 = (bf16[256,256]{1,0:T(8,128)(2,1)}, bf16[256,256]{1,0:T(8,128)(2,1)}) custom-call(s32[5]{0:T(128)} %stack.32.me, bf16[256,1024]{1,0:T(8,128)(2,1)} %x_ref.3, f32[1,1024]{1,0:T(1,128)} %bitcast.51, bf16[1024,256]{1,0:T(8,128)(2,1)} %wq_ref.1, bf16[1024,128]{1,0:T(8,128)(2,1)} %wk_ref.1, bf16[1024,128]{1,0:T(8,128)(2,1)} %wv_ref.1, ...), custom_call_target="tpu_custom_call" | custom-call | tf_op jit(solution)/shard_map/start/pallas_call | solution.py:426
  18.4 2.8 %collective-permute-start.5 = (bf16[256,1024]{1,0:T(8,128)(2,1)}, bf16[256,1024]{1,0:T(8,128)(2,1)}, u32[]{:S(2)}, u32[]{:S(2)}) collective-permute-start(bf16[256,1024]{1,0:T(8,128)(2,1)} %wo_ref.1), channel_id=1, source_target_pairs={{0,2},{2,0},{1,3},{3,1},{4,6},{6,4},{5,7},{7,5},{8,10},{10,8},{9,1... | collective-permute-start | bytes 1572872 | tf_op jit(solution)/shard_map/ppermute | solution.py:695
  24.5 7.8 %all-to-all-start = ((bf16[16,512,128]{2,1,0:T(8,128)(2,1)}), bf16[16,512,128]{2,1,0:T(8,128)(2,1)S(1)}, u32[]{:S(2)}, u32[]{:S(2)}) async-start(bf16[16,512,128]{2,1,0:T(8,128)(2,1)} %broadcast_in_dim.62), calls=%async_computation | async-start | bytes 4194304 | tf_op jit(solution)/shard_map/all_to_all | solution.py:689
  34.6 8.0 %collective-permute-done.2 = f32[256,8]{0,1:T(8,128)S(1)} collective-permute-done((f32[256,8]{0,1:T(8,128)S(1)}, f32[256,8]{0,1:T(8,128)S(1)}, u32[]{:S(2)}, u32[]{:S(2)}) %collective-permute-start.2) | collective-permute-done | bytes 8224 | tf_op jit(solution)/shard_map/ppermute | solution.py:39
  50.6 10.4 %all-to-all-done = bf16[16,512,128]{2,1,0:T(8,128)(2,1)S(1)} async-done(((bf16[16,512,128]{2,1,0:T(8,128)(2,1)}), bf16[16,512,128]{2,1,0:T(8,128)(2,1)S(1)}, u32[]{:S(2)}, u32[]{:S(2)}) %all-to-all-start) | async-done | bytes 2097184 | tf_op jit(solution)/shard_map/all_to_all | solution.py:689
  61.8 11.2 %attend.1 = (bf16[512,128]{1,0:T(8,128)(2,1)S(1)}, f32[4,64,256]{2,1,0:T(8,128)S(1)}, f32[4,1,256]{2,1,0:T(1,128)S(1)}, bf16[8,1024,128]{2,1,0:T(8,128)(2,1)S(1)}, bf16[8,128,1024]{2,1,0:T(8,128)(2,1)S(1)}) custom-call(s32[4]{0:T(128)S(1)} %and_select_fusion.2.place, s32[64]{0:T(128)S(1)} %pad_add_fusion.slot, ...), custom_call_target="tpu_custom_call" | custom-call | flops 20000000000 | bytes 8000000 | tf_op jit(solution)/shard_map/attend/pallas_call | solution.py:146
  77.4 3.5 %all-to-all-start.1 = ((bf16[4,512,128]{2,1,0:T(8,128)(2,1)}), bf16[4,512,128]{2,1,0:T(8,128)(2,1)S(1)}, u32[]{:S(2)}, u32[]{:S(2)}) async-start(bf16[4,512,128]{2,1,0:T(8,128)(2,1)} %broadcast_in_dim.63), calls=%async_computation.1 | async-start | bytes 1048576 | tf_op jit(solution)/shard_map/all_to_all | solution.py:721
  83.3 4.2 %all-to-all-done.1.o_ref = bf16[4,512,128]{2,1,0:T(8,128)(2,1)S(1)} async-done(((bf16[4,512,128]{2,1,0:T(8,128)(2,1)}), bf16[4,512,128]{2,1,0:T(8,128)(2,1)S(1)}, u32[]{:S(2)}, u32[]{:S(2)}) %all-to-all-start.1) | async-done | bytes 524320 | tf_op jit(solution)/shard_map/all_to_all | solution.py:721
  87.5 4.7 %collective-permute-start.7 = (bf16[4,512,128]{2,1,0:T(8,128)(2,1)S(1)}, bf16[4,512,128]{2,1,0:T(8,128)(2,1)S(1)}, u32[]{:S(2)}, u32[]{:S(2)}) collective-permute-start(bf16[4,512,128]{2,1,0:T(8,128)(2,1)S(1)} %all-to-all-done.1.o_ref), channel_id=1, source_target_pairs={{0,1},{1,0},{2,3},{3,2},{4,5},{5,4},{6,7},{7,6},{8,9},{9,8},{10,11... | collective-permute-start | bytes 1572872 | tf_op jit(solution)/shard_map/ppermute | solution.py:726
  94.5 21.6 %experts.1 = (f32[64,1024]{1,0:T(8,128)}, bf16[512,1024]{1,0:T(8,128)(2,1)}, f32[64,128]{1,0:T(8,128)}, bf16[4,64,1152]{2,1,0:T(8,128)(2,1)}, bf16[4,64,1152]{2,...) custom-call(s32[5]{0:T(128)} %stack.32.me, ...), custom_call_target="tpu_custom_call" | custom-call | flops 15000000512 | bytes 20000000 | tf_op jit(solution)/shard_map/experts/pallas_call | solution.py:377
  118.7 11.8 %all_to_all.35.part_ref = bf16[4,64,1152]{2,1,0:T(8,128)(2,1)S(1)} all-to-all(bf16[4,64,1152]{2,1,0:T(8,128)(2,1)S(1)} %add_convert_fusion), channel_id=1, replica_groups=mesh['z'=4,'y'=4,'xl'=2,'xh'=2,'c'=2] {'xl','xh'}, dimensions={0} | all-to-all | bytes 1179648 | tf_op jit(solution)/shard_map/all_to_all | solution.py:738
  131.7 10.7 %all_to_all.36.full_ref = bf16[4,64,1152]{2,1,0:T(8,128)(2,1)S(1)} all-to-all(bf16[4,64,1152]{2,1,0:T(8,128)(2,1)S(1)} %middle.1), channel_id=1, replica_groups=mesh['z'=4,'y'=4,'xl'=2,'xh'=2,'c'=2] {'xl','xh'}, dimensions={0} | all-to-all | bytes 1179648 | tf_op jit(solution)/shard_map/all_to_all | solution.py:741
  142.4 2.7 %collective-permute-start.9 = (bf16[4,64,1152]{2,1,0:T(8,128)(2,1)S(1)}, bf16[4,64,1152]{2,1,0:T(8,128)(2,1)S(1)}, u32[]{:S(2)}, u32[]{:S(2)}) collective-permute-start(bf16[4,64,1152]{2,1,0:T(8,128)(2,1)S(1)} %all_to_all.36.full_ref), channel_id=1, source_target_pairs={{0,1},{1,0},{2,3},{3,2},{4,5},{5,4},{6,7},{7,6},{8,9},{9,8},{10,11... | collective-permute-start | bytes 1769480 | tf_op jit(solution)/shard_map/ppermute | solution.py:742
  147.5 15.0 %attend_back.1 = (bf16[512,128]{1,0:T(8,128)(2,1)S(1)}, bf16[64,128,128]{2,1,0:T(8,128)(2,1)S(1)}, bf16[512,1024]{1,0:T(8,128)(2,1)S(1)}, bf16[512,128]{1,0:T(8,128)(2,1)S(1)}) custom-call(s32[4]{0:T(128)S(1)} %and_select_fusion.2.place, s32[64]{0:T(128)S(1)} %pad_add_fusion.slot, s32[5]{0:T(128)S(1)} %copy-done.20, bf16[512,128]{1,0:T(8,128)(2,1)S(1)} %copy-done.17, ...), custom_call_target="tpu_custom_call" | custom-call | flops 30000001024 | bytes 8000000 | tf_op jit(solution)/shard_map/attend_back/pallas_call | solution.py:254
  166.3 4.5 %all-to-all-start.4 = ((bf16[16,512,128]{2,1,0:T(8,128)(2,1)}), bf16[16,512,128]{2,1,0:T(8,128)(2,1)S(1)}, u32[]{:S(2)}, u32[]{:S(2)}) async-start(bf16[16,512,128]{2,1,0:T(8,128)(2,1)} %bitcast.48), calls=%async_computation.4 | async-start | bytes 4194304 | tf_op jit(solution)/shard_map/all_to_all | solution.py:766
  171.7 2.4 convolution_convert_fusion.1
  195.3 3.0 %collective-permute-done.16.last_ref = bf16[64,1024]{1,0:T(8,128)(2,1)} collective-permute-done((bf16[64,1024]{1,0:T(8,128)(2,1)S(1)}, bf16[64,1024]{1,0:T(8,128)(2,1)}, u32[]{:S(2)}, u32[]{:S(2)}) %collective-permute-start.16) | collective-permute-done | bytes 131104 | tf_op jit(solution)/shard_map/ppermute | solution.py:701
  198.3 4.3 %all-to-all-done.4.part_ref = bf16[16,512,128]{2,1,0:T(8,128)(2,1)S(1)} async-done(((bf16[16,512,128]{2,1,0:T(8,128)(2,1)}), bf16[16,512,128]{2,1,0:T(8,128)(2,1)S(1)}, u32[]{:S(2)}, u32[]{:S(2)}) %all-to-all-start.4) | async-done | bytes 2097184 | tf_op jit(solution)/shard_map/all_to_all | solution.py:766
  204.6 10.2 %all_to_all.37.m_ref = bf16[4,256,256]{2,1,0:T(8,128)(2,1)S(1)} all-to-all(bf16[4,256,256]{2,1,0:T(8,128)(2,1)S(1)} %bitcast.57), channel_id=1, replica_groups=mesh['z'=4,'y'=4,'xl'=2,'xh'=2,'c'=2] {'xl','xh'}, dimensions={0} | all-to-all | bytes 1048576 | tf_op jit(solution)/shard_map/all_to_all | solution.py:784
  214.8 2.4 collective-permute-start.20
  218.8 5.2 %finish.1 = (bf16[256,1024]{1,0:T(8,128)(2,1)}, bf16[1024,512]{1,0:T(8,128)(2,1)S(1)}) custom-call(s32[5]{0:T(128)S(1)} %copy-done.20, bf16[4,256,256]{2,1,0:T(8,128)(2,1)S(1)} %all_to_all.37.m_ref, bf16[4,256,256]{2,1,0:T(8,128)(2,1)S(1)} %collective-permute-done.20.o_ref, bf16[1024,512]{1,0:T(8,128)(2,1)} %pad_maximum_fusion.1.w0, ...), custom_call_target="tpu_custom_call" | custom-call | tf_op jit(solution)/shard_map/finish/pallas_call | solution.py:559
  225.0 4.1 %all-to-all-start.6 = ((bf16[32,32,512]{2,1,0:T(8,128)(2,1)}), bf16[32,32,512]{2,1,0:T(8,128)(2,1)S(1)}, u32[]{:S(2)}, u32[]{:S(2)}) async-start(bf16[32,32,512]{2,1,0:T(8,128)(2,1)} %bitcast.50), calls=%async_computation.7 | async-start | bytes 2097152 | tf_op jit(solution)/shard_map/all_to_all | solution.py:810
  232.4 13.7 %all-to-all-done.6.part_ref = bf16[32,32,512]{2,1,0:T(8,128)(2,1)S(1)} async-done(((bf16[32,32,512]{2,1,0:T(8,128)(2,1)}), bf16[32,32,512]{2,1,0:T(8,128)(2,1)S(1)}, u32[]{:S(2)}, u32[]{:S(2)}) %all-to-all-start.6) | async-done | bytes 1048608 | tf_op jit(solution)/shard_map/all_to_all | solution.py:810
  246.1 2.8 %unpack.1 = (f32[32,256]{1,0:T(8,128)}, f32[32,128]{1,0:T(8,128)}, f32[32,128]{1,0:T(8,128)}, f32[32,256]{1,0:T(8,128)}, f32[16,32]{1,0:T(8,128)}, /*index=5*/f3...) custom-call(s32[5]{0:T(128)S(1)} %copy-done.20, ...), custom_call_target="tpu_custom_call" | custom-call | tf_op jit(solution)/shard_map/unpack/pallas_call | solution.py:626
  (181 shorter events, 70.3 us)
Async XLA Ops:
  14.9 6.8 %collective-permute-start = (bf16[256,256]{1,0:T(8,128)(2,1)}, bf16[256,256]{1,0:T(8,128)(2,1)S(1)}, u32[]{:S(2)}, u32[]{:S(2)}) collective-permute-start(bf16[256,256]{1,0:T(8,128)(2,1)} %get-tuple-element.75), channel_id=1, source_target_pairs={{0,4},{4,0},{1,5},{5,1},{2,6},{6,2},{3,7},{7,3},{8,12},{12,8},{9,1... | collective-permute-start | bytes 393224 | tf_op jit(solution)/shard_map/ppermute | solution.py:683
  17.0 29.8 %collective-permute-start.1 = (bf16[256,1024]{1,0:T(8,128)(2,1)S(1)}, bf16[256,1024]{1,0:T(8,128)(2,1)}, u32[]{:S(2)}, u32[]{:S(2)}) collective-permute-start(bf16[256,1024]{1,0:T(8,128)(2,1)S(1)} %copy-done), channel_id=1, source_target_pairs={{0,4},{4,0},{1,5},{5,1},{2,6},{6,2},{3,7},{7,3},{8,12},{12,8},{9,1... | collective-permute-start | bytes 1572872 | tf_op jit(solution)/shard_map/ppermute | solution.py:39
  17.1 59.4 %collective-permute-start.4 = (bf16[256,1024]{1,0:T(8,128)(2,1)}, bf16[256,1024]{1,0:T(8,128)(2,1)}, u32[]{:S(2)}, u32[]{:S(2)}) collective-permute-start(bf16[256,1024]{1,0:T(8,128)(2,1)} %wo_ref.1), channel_id=1, source_target_pairs={{0,1},{1,0},{2,3},{3,2},{4,5},{5,4},{6,7},{7,6},{8,9},{9,8},{10,11... | collective-permute-start | bytes 1572872 | tf_op jit(solution)/shard_map/ppermute | solution.py:694
  18.4 26.8 %collective-permute-start.5 = (bf16[256,1024]{1,0:T(8,128)(2,1)}, bf16[256,1024]{1,0:T(8,128)(2,1)}, u32[]{:S(2)}, u32[]{:S(2)}) collective-permute-start(bf16[256,1024]{1,0:T(8,128)(2,1)} %wo_ref.1), channel_id=1, source_target_pairs={{0,2},{2,0},{1,3},{3,1},{4,6},{6,4},{5,7},{7,5},{8,10},{10,8},{9,1... | collective-permute-start | bytes 1572872 | tf_op jit(solution)/shard_map/ppermute | solution.py:695
  21.2 21.4 %collective-permute-start.2 = (f32[256,8]{0,1:T(8,128)S(1)}, f32[256,8]{0,1:T(8,128)S(1)}, u32[]{:S(2)}, u32[]{:S(2)}) collective-permute-start(f32[256,8]{0,1:T(8,128)S(1)} %convert_element_type.80), channel_id=1, source_target_pairs={{0,4},{4,0},{1,5},{5,1},{2,6},{6,2},{3,7},{7,3},{8,12},{12,8},{9,1... | collective-permute-start | bytes 24584 | tf_op jit(solution)/shard_map/ppermute | solution.py:39
  24.5 36.5 %all-to-all-start = ((bf16[16,512,128]{2,1,0:T(8,128)(2,1)}), bf16[16,512,128]{2,1,0:T(8,128)(2,1)S(1)}, u32[]{:S(2)}, u32[]{:S(2)}) async-start(bf16[16,512,128]{2,1,0:T(8,128)(2,1)} %broadcast_in_dim.62), calls=%async_computation | async-start | bytes 4194304 | tf_op jit(solution)/shard_map/all_to_all | solution.py:689
  45.2 31.3 %collective-permute-start.6 = (bf16[256,1024]{1,0:T(8,128)(2,1)}, bf16[256,1024]{1,0:T(8,128)(2,1)}, u32[]{:S(2)}, u32[]{:S(2)}) collective-permute-start(bf16[256,1024]{1,0:T(8,128)(2,1)} %collective-permute-done.5.wo2), channel_id=1, source_target_pairs={{0,1},{1,0},{2,3},{3,2},{4,5},{5,4},{6,7},{7,6},{8,9},{9,8},{10,11... | collective-permute-start | bytes 1572872 | tf_op jit(solution)/shard_map/ppermute | solution.py:696
  60.9 15.6 %collective-permute-start.3 = (bf16[256,1024]{1,0:T(8,128)(2,1)}, bf16[256,1024]{1,0:T(8,128)(2,1)}, u32[]{:S(2)}, u32[]{:S(2)}) collective-permute-start(bf16[256,1024]{1,0:T(8,128)(2,1)} %param.15), channel_id=1, source_target_pairs={{0,4},{4,0},{1,5},{5,1},{2,6},{6,2},{3,7},{7,3},{8,12},{12,8},{9,1... | collective-permute-start | bytes 1572872 | tf_op jit(solution)/shard_map/ppermute | solution.py:711
  77.4 10.1 %all-to-all-start.1 = ((bf16[4,512,128]{2,1,0:T(8,128)(2,1)}), bf16[4,512,128]{2,1,0:T(8,128)(2,1)S(1)}, u32[]{:S(2)}, u32[]{:S(2)}) async-start(bf16[4,512,128]{2,1,0:T(8,128)(2,1)} %broadcast_in_dim.63), calls=%async_computation.1 | async-start | bytes 1048576 | tf_op jit(solution)/shard_map/all_to_all | solution.py:721
  80.9 121.8 %reduce-scatter.3.cloned.1.call-start = ((), (), s32[]{:S(2)}) async-start(), calls=%async_computation.9 | async-start | bytes 7864320 | tf_op jit(solution)/shard_map/reduce_scatter | solution.py:739
  145.1 26.6 %collective-permute-start.10 = (bf16[4,64,1024]{2,1,0:T(8,128)(2,1)}, bf16[4,64,1024]{2,1,0:T(8,128)(2,1)}, u32[]{:S(2)}, u32[]{:S(2)}) collective-permute-start(bf16[4,64,1024]{2,1,0:T(8,128)(2,1)} %get-tuple-element.104), channel_id=1, source_target_pairs={{0,1},{1,0},{2,3},{3,2},{4,5},{5,4},{6,7},{7,6},{8,9},{9,8},{10,11... | collective-permute-start | bytes 1572872 | tf_op jit(solution)/shard_map/ppermute | solution.py:750
  145.1 30.5 %collective-permute-start.18 = (bf16[1024,512]{1,0:T(8,128)(2,1)}, bf16[1024,512]{1,0:T(8,128)(2,1)}, u32[]{:S(2)}, u32[]{:S(2)}) collective-permute-start(bf16[1024,512]{1,0:T(8,128)(2,1)} %pad_maximum_fusion.1.w0), channel_id=1, source_target_pairs={{0,2},{2,0},{1,3},{3,1},{4,6},{6,4},{5,7},{7,5},{8,10},{10,8},{9,1... | collective-permute-start | bytes 3145736 | tf_op jit(solution)/shard_map/ppermute | solution.py:695
  166.3 36.4 %all-to-all-start.4 = ((bf16[16,512,128]{2,1,0:T(8,128)(2,1)}), bf16[16,512,128]{2,1,0:T(8,128)(2,1)S(1)}, u32[]{:S(2)}, u32[]{:S(2)}) async-start(bf16[16,512,128]{2,1,0:T(8,128)(2,1)} %bitcast.48), calls=%async_computation.4 | async-start | bytes 4194304 | tf_op jit(solution)/shard_map/all_to_all | solution.py:766
  170.8 58.3 %reduce-scatter.5.cloned.1.call-start = ((), (), s32[]{:S(2)}) async-start(), calls=%async_computation.10 | async-start | bytes 1966080 | tf_op jit(solution)/shard_map/reduce_scatter | solution.py:779
  170.9 27.4 %collective-permute-start.17 = (bf16[1024,512]{1,0:T(8,128)(2,1)}, bf16[1024,512]{1,0:T(8,128)(2,1)}, u32[]{:S(2)}, u32[]{:S(2)}) collective-permute-start(bf16[1024,512]{1,0:T(8,128)(2,1)} %pad_maximum_fusion.1.w0), channel_id=1, source_target_pairs={{0,1},{1,0},{2,3},{3,2},{4,5},{5,4},{6,7},{7,6},{8,9},{9,8},{10,11... | collective-permute-start | bytes 3145736 | tf_op jit(solution)/shard_map/ppermute | solution.py:694
  175.5 22.7 %collective-permute-start.19 = (bf16[1024,512]{1,0:T(8,128)(2,1)}, bf16[1024,512]{1,0:T(8,128)(2,1)}, u32[]{:S(2)}, u32[]{:S(2)}) collective-permute-start(bf16[1024,512]{1,0:T(8,128)(2,1)} %collective-permute-done.18.w2), channel_id=1, source_target_pairs={{0,1},{1,0},{2,3},{3,2},{4,5},{5,4},{6,7},{7,6},{8,9},{9,8},{10,11... | collective-permute-start | bytes 3145736 | tf_op jit(solution)/shard_map/ppermute | solution.py:696
  176.5 8.5 %collective-permute-start.13 = (bf16[64,1024]{1,0:T(8,128)(2,1)}, bf16[64,1024]{1,0:T(8,128)(2,1)S(1)}, u32[]{:S(2)}, u32[]{:S(2)}) collective-permute-start(bf16[64,1024]{1,0:T(8,128)(2,1)} %get-tuple-element.141), channel_id=1, source_target_pairs={{0,6},{6,0},{2,4},{4,2},{1,7},{7,1},{3,5},{5,3},{8,14},{14,8},{10,... | collective-permute-start | bytes 393224 | tf_op jit(solution)/shard_map/ppermute | solution.py:761
  177.4 7.6 %collective-permute-start.12 = (bf16[64,1024]{1,0:T(8,128)(2,1)}, bf16[64,1024]{1,0:T(8,128)(2,1)}, u32[]{:S(2)}, u32[]{:S(2)}) collective-permute-start(bf16[64,1024]{1,0:T(8,128)(2,1)} %get-tuple-element.142), channel_id=1, source_target_pairs={{0,2},{2,0},{1,3},{3,1},{4,6},{6,4},{5,7},{7,5},{8,10},{10,8},{9,1... | collective-permute-start | bytes 393224 | tf_op jit(solution)/shard_map/ppermute | solution.py:760
  178.6 7.2 %collective-permute-start.11 = (bf16[64,1024]{1,0:T(8,128)(2,1)}, bf16[64,1024]{1,0:T(8,128)(2,1)}, u32[]{:S(2)}, u32[]{:S(2)}) collective-permute-start(bf16[64,1024]{1,0:T(8,128)(2,1)} %get-tuple-element.140), channel_id=1, source_target_pairs={{0,4},{4,0},{1,5},{5,1},{2,6},{6,2},{3,7},{7,3},{8,12},{12,8},{9,1... | collective-permute-start | bytes 393224 | tf_op jit(solution)/shard_map/ppermute | solution.py:759
  187.0 6.9 %collective-permute-start.14 = (bf16[64,1024]{1,0:T(8,128)(2,1)S(1)}, bf16[64,1024]{1,0:T(8,128)(2,1)}, u32[]{:S(2)}, u32[]{:S(2)}) collective-permute-start(bf16[64,1024]{1,0:T(8,128)(2,1)S(1)} %fusion.8.own_ref), channel_id=1, source_target_pairs={{0,1},{1,0},{2,3},{3,2},{4,5},{5,4},{6,7},{7,6},{8,9},{9,8},{10,11... | collective-permute-start | bytes 393224 | tf_op jit(solution)/shard_map/ppermute | solution.py:701
  188.6 6.7 %collective-permute-start.15 = (bf16[64,1024]{1,0:T(8,128)(2,1)S(1)}, bf16[64,1024]{1,0:T(8,128)(2,1)}, u32[]{:S(2)}, u32[]{:S(2)}) collective-permute-start(bf16[64,1024]{1,0:T(8,128)(2,1)S(1)} %fusion.8.own_ref), channel_id=1, source_target_pairs={{0,2},{2,0},{1,3},{3,1},{4,6},{6,4},{5,7},{7,5},{8,10},{10,8},{9,1... | collective-permute-start | bytes 393224 | tf_op jit(solution)/shard_map/ppermute | solution.py:701
  189.7 8.5 %collective-permute-start.16 = (bf16[64,1024]{1,0:T(8,128)(2,1)S(1)}, bf16[64,1024]{1,0:T(8,128)(2,1)}, u32[]{:S(2)}, u32[]{:S(2)}) collective-permute-start(bf16[64,1024]{1,0:T(8,128)(2,1)S(1)} %fusion.8.own_ref), channel_id=1, source_target_pairs={{0,3},{3,0},{1,2},{2,1},{4,7},{7,4},{5,6},{6,5},{8,11},{11,8},{9,1... | collective-permute-start | bytes 393224 | tf_op jit(solution)/shard_map/ppermute | solution.py:701
  225.0 21.1 %all-to-all-start.6 = ((bf16[32,32,512]{2,1,0:T(8,128)(2,1)}), bf16[32,32,512]{2,1,0:T(8,128)(2,1)S(1)}, u32[]{:S(2)}, u32[]{:S(2)}) async-start(bf16[32,32,512]{2,1,0:T(8,128)(2,1)} %bitcast.50), calls=%async_computation.7 | async-start | bytes 2097152 | tf_op jit(solution)/shard_map/all_to_all | solution.py:810
  231.1 15.0 %collective-permute-start.21 = (bf16[2,48,1024]{2,1,0:T(8,128)(2,1)S(1)}, bf16[2,48,1024]{2,1,0:T(8,128)(2,1)S(1)}, u32[]{:S(2)}, u32[]{:S(2)}) collective-permute-start(bf16[2,48,1024]{2,1,0:T(8,128)(2,1)S(1)} %get-tuple-element.143), channel_id=1, source_target_pairs={{0,4},{4,0},{1,5},{5,1},{2,6},{6,2},{3,7},{7,3},{8,12},{12,8},{9,1... | collective-permute-start | bytes 589832 | tf_op jit(solution)/shard_map/ppermute | solution.py:808
  (44 other events, 526.2 us)
Sparse Core Ops, SparseCore 0:
  116.3 62.1 reduce-scatter.2
  202.8 23.2 reduce-scatter.4
